TPU v7x, 512 devices: a whole 4x8x8 slice. The times are simulated.
512 devices in a mesh: row: 32 (over y, x), col: 16 (over z, core).
Axes of the slice: x: 4, y: 8, z: 8, core: 2. Of those that a mesh axis runs over, the one named last changes fastest.
Arguments:
- trailing_grad: float32 [16384, 16384], P('row', 'col'), as said below
- factor_rows: float32 [16384, 1024], P(('row', 'col')), may hold values from -0.046875 to 0.046875
- factor_grad: float32 [16384, 1024], P(('row', 'col')), may hold values from -6 to 6
- diag_factor: float32 [2, 512, 512], P(None, 'row'), as said below
- cross_factor: float32 [512, 512], P('row'), may hold values from -0.25 to 0.25
- cross_grad: float32 [512, 1024], P('row', 'col'), may hold values from -6 to 6
- corner_grad: float32 [512, 512], P('row', 'col'), may hold values from -6 to 6
Outputs:
- rows_grad: float32 [16384, 1024], P(('row', 'col'))
- blocks_grad: float32 [2, 512, 512], P(None, 'row', 'col')
- coupling_grad: float32 [512, 512], P('row', 'col')
Inputs may be any that keep to these rules, and one draw needn't show every extreme that they name: `trailing_grad`: symmetric. `diag_factor`: each of the two 512 x 512 blocks is lower triangular with its diagonal between 1 and 2.
All inputs are finite; a program needn't handle non-finite values.
Results may differ from a plain program's by a relative error of at most 0.00018.
Values sent between devices are 32-bit elements; how exact they have to be, the bound alone decides.
A program may use at most 64 MiB of HBM per device.

v0:
```python
import jax
import jax.numpy as jnp
from jax import lax
from jax.sharding import PartitionSpec as P

highest = lax.Precision.HIGHEST


def broadcast(value, axis, source):
    kept = jnp.where(lax.axis_index(axis) == source, value, 0).astype(value.dtype)
    return lax.psum(kept, axis)


def matmul(left, right):
    return jnp.dot(left, right, precision=highest, preferred_element_type=jnp.float32)


def inner_t(left, right):
    return lax.dot_general(
        left, right, (((0,), (0,)), ((), ())), precision=highest, preferred_element_type=jnp.float32
    )


def lower_inverse(factor):
    identity = jnp.eye(factor.shape[0], dtype=jnp.float32)
    return lax.linalg.triangular_solve(factor, identity, left_side=True, lower=True)


def block_adjoint(factor, inverse, lowered_grad):
    identity = jnp.eye(factor.shape[0], dtype=jnp.float32)
    product = inner_t(factor, lowered_grad)
    lowered = jnp.tril(product) - 0.5 * product * identity
    return 0.5 * inner_t(inverse, matmul(lowered + lowered.T, inverse))


def per_device(
    trailing_grad, factor_rows, factor_grad, diag_factor, cross_factor, cross_grad, corner_grad
):
    row_count = lax.axis_size("row")
    col_count = lax.axis_size("col")
    row_place = lax.axis_index("row")
    col_place = lax.axis_index("col")
    local_rows, full_width = factor_rows.shape
    panel_width = full_width // 2
    per_column = row_count // col_count
    row_band = lax.all_gather(factor_rows, "col", axis=0, tiled=True)
    members = []
    for member in range(per_column):
        members.append(broadcast(row_band, "row", col_place * per_column + member))
    column_rows = jnp.stack(members, 0)
    tile_rows = trailing_grad
    tile_rows = tile_rows.reshape(
        local_rows * lax.axis_size("col"), per_column, col_count * local_rows
    )
    product = lax.psum_scatter(
        jnp.einsum(
            "rjm,jmn->rn",
            tile_rows,
            column_rows,
            precision=highest,
            preferred_element_type=jnp.float32,
        ),
        "col",
        scatter_dimension=0,
        tiled=True,
    )
    diag_full, cross_full = (
        lax.all_gather(diag_factor, "row", axis=1, tiled=True),
        lax.all_gather(cross_factor, "row", axis=0, tiled=True),
    )
    first_inverse = lower_inverse(diag_full[0])
    second_inverse = lower_inverse(diag_full[1])
    second_adjoint = matmul(
        factor_grad[:, panel_width:] - 2.0 * product[:, panel_width:], second_inverse
    )
    piece_rows, piece_cols = cross_grad.shape
    own_panel = jnp.zeros((panel_width, full_width), jnp.float32)
    own_panel = lax.dynamic_update_slice(
        own_panel, cross_grad, (row_place * piece_rows, col_place * piece_cols)
    )
    panel_part = lax.psum_scatter(
        own_panel - inner_t(second_adjoint, factor_rows), "row", scatter_dimension=0, tiled=True
    )
    panel_part = lax.psum(panel_part, "col")
    panel_total = lax.all_gather(panel_part, "row", axis=0, tiled=True)
    second_block = block_adjoint(
        diag_full[1], second_inverse, jnp.tril(panel_total[:, panel_width:])
    )
    coupling = matmul(
        panel_total[:, :panel_width] - 2.0 * matmul(second_block, cross_full), first_inverse
    )
    first_adjoint = matmul(
        factor_grad[:, :panel_width]
        - 2.0 * product[:, :panel_width]
        - matmul(second_adjoint, cross_full),
        first_inverse,
    )
    corner_rows, corner_cols = corner_grad.shape
    own_corner = jnp.zeros((panel_width, panel_width), jnp.float32)
    own_corner = lax.dynamic_update_slice(
        own_corner, corner_grad, (row_place * corner_rows, col_place * corner_cols)
    )
    corner_part = lax.psum_scatter(
        own_corner - inner_t(first_adjoint, factor_rows[:, :panel_width]),
        "row",
        scatter_dimension=0,
        tiled=True,
    )
    corner_part = lax.psum(corner_part, "col")
    corner_total = lax.all_gather(corner_part, "row", axis=0, tiled=True)
    first_grad = jnp.tril(corner_total - inner_t(coupling, cross_full))
    first_block = block_adjoint(diag_full[0], first_inverse, first_grad)
    rows_grad = jnp.concatenate([first_adjoint, second_adjoint], 1)
    both_blocks = jnp.stack([first_block, second_block])
    blocks_grad = lax.dynamic_slice(
        both_blocks,
        (0, row_place * corner_rows, col_place * corner_cols),
        (2, corner_rows, corner_cols),
    )
    coupling_grad = lax.dynamic_slice(
        coupling, (row_place * corner_rows, col_place * corner_cols), (corner_rows, corner_cols)
    )
    return (rows_grad, blocks_grad, coupling_grad)


def solution(mesh):
    return jax.shard_map(
        per_device,
        mesh=mesh,
        in_specs=(
            P("row", "col"),
            P(("row", "col"), None),
            P(("row", "col"), None),
            P(None, "row", None),
            P("row", None),
            P("row", "col"),
            P("row", "col"),
        ),
        out_specs=(P(("row", "col"), None), P(None, "row", "col"), P("row", "col")),
        check_vma=False,
    )
```

profile of v0, /device:TPU:1, one launch (start us, length us, event | category | flops | bytes accessed | tf_op | source)
XLA Modules:
  0.0 1217.5 jit_solution(6141983328008660040)
XLA Ops:
  8.0 51.3 %all-gather.6.cloned.1.call-done = f32[512,1024]{1,0:T(8,128)} async-done(((f32[32,1024]{1,0:T(8,128)}), f32[512,1024]{1,0:T(8,128)}) %all-gather.6.cloned.1.call-update) | async-done | bytes 2097168 | tf_op jit(solution)/shard_map/all_gather | solution.py:46
  61.2 2.7 select_bitcast_fusion.1
  64.7 169.7 %all-reduce.6.cloned.1.call-done = (f32[1,512,1024]{1,2,0:T(8,128)}, f32[1,512,1024]{1,2,0:T(8,128)}) async-done(((f32[1,512,1024]{1,2,0:T(8,128)}, f32[1,512,1024]{1,2,0:T(8,128)}), (f32[1,512,1024]{1,2,0:T(8,128)}, f32[1,512,1024]{1,2,0:T(8,128)})) %all-reduce.6.cloned.1.call-update) | async-done | bytes 4194320 | tf_op jit(solution)/shard_map/psum | solution.py:11
  234.5 9.3 fusion.6
  249.7 68.0 %all-gather.8.cloned.1.call-done = f32[2,512,512]{2,1,0:T(8,128)} async-done(((f32[2,16,512]{2,1,0:T(8,128)}), f32[2,512,512]{2,1,0:T(8,128)}) %all-gather.8.cloned.1.call-update) | async-done | bytes 2097168 | tf_op jit(solution)/shard_map/all_gather | solution.py:68
  317.7 3.2 fusion.27
  320.9 11.5 while.4
  332.4 39.9 %custom-call.4 = f32[4,128,128]{1,2,0:T(8,128)} custom-call(f32[4,128,128]{2,1,0:T(8,128)S(1)} %get-tuple-element.18), custom_call_target="InvertDiagBlocksLowerTriangular" | custom-call | tf_op jit(solution)/shard_map/triangular_solve/custom-call.1 | solution.py:26
  388.0 3.2 convolution_subtract_fusion
  391.2 2.9 copy.41
  396.2 11.6 while.5
  407.8 39.3 %custom-call.5 = f32[4,128,128]{1,2,0:T(8,128)S(1)} custom-call(f32[4,128,128]{2,1,0:T(8,128)S(1)} %get-tuple-element.19), custom_call_target="InvertDiagBlocksLowerTriangular" | custom-call | tf_op jit(solution)/shard_map/triangular_solve/custom-call.1 | solution.py:26
  455.0 8.6 all-gather.10.cloned.1.call-done
  463.7 3.0 convolution_subtract_fusion.9
  467.4 220.3 %reduce-scatter.14.cloned.1.call-done = f32[16,1024]{1,0:T(8,128)} async-done(((f32[512,1024]{1,0:T(8,128)}), f32[16,1024]{1,0:T(8,128)}) %reduce-scatter.14.cloned.1.call-update) | async-done | bytes 65552
  691.8 117.9 %all-reduce.4.cloned.1.call-done = f32[16,1024]{0,1:T(8,128)} async-done(((f32[16,1024]{0,1:T(8,128)}), f32[16,1024]{0,1:T(8,128)}) %all-reduce.4.cloned.1.call-update) | async-done | bytes 65552 | tf_op jit(solution)/shard_map/psum | solution.py:84
  811.6 217.3 %reduce-scatter.12.cloned.1.call-done = f32[16,512]{1,0:T(8,128)} async-done(((f32[512,512]{1,0:T(8,128)}), f32[16,512]{1,0:T(8,128)}) %reduce-scatter.12.cloned.1.call-update) | async-done | bytes 32784
  1029.8 52.4 %psum.30 = f32[16,512]{0,1:T(8,128)S(1)} all-reduce(f32[16,512]{0,1:T(8,128)S(1)} %copy.40), channel_id=1, replica_groups=mesh['row'=32,'col'=16] {'col'}, use_global_device_ids=true, to_apply=%region_4.0 | all-reduce | flops 8192 | bytes 65536 | tf_op jit(solution)/shard_map/psum | solution.py:109
  1083.6 32.4 %all-gather.14.cloned.1.call-done = f32[512,1024]{1,0:T(8,128)} async-done(((f32[16,1024]{1,0:T(8,128)}), f32[512,1024]{1,0:T(8,128)}) %all-gather.14.cloned.1.call-update) | async-done | bytes 2097168 | tf_op jit(solution)/shard_map/all_gather | solution.py:85
  1116.0 4.1 fusion.14
  1122.8 3.3 fusion.23
  1133.5 64.2 %all-gather.12.cloned.1.call-done = f32[512,512]{1,0:T(8,128)} async-done(((f32[16,512]{1,0:T(8,128)}), f32[512,512]{1,0:T(8,128)}) %all-gather.12.cloned.1.call-update) | async-done | bytes 1048592 | tf_op jit(solution)/shard_map/all_gather | solution.py:110
  1197.7 3.5 fusion.12
  1204.7 3.2 fusion.17
  (162 shorter events, 82.4 us)
Async XLA Ops:
  7.2 52.1 %all-gather.6.cloned.1.call-start = ((), (), s32[]{:S(2)}) async-start(), calls=%async_computation.3 | async-start | bytes 2228224 | tf_op jit(solution)/shard_map/all_gather | solution.py:46
  7.9 226.6 %all-reduce.6.cloned.1.call-start = ((), (), s32[]{:S(2)}) async-start(), calls=%async_computation.12 | async-start | bytes 8388608 | tf_op jit(solution)/shard_map/psum | solution.py:11
  63.9 253.8 %all-gather.8.cloned.1.call-start = ((), (), s32[]{:S(2)}) async-start(), calls=%async_computation.4 | async-start | bytes 2162688 | tf_op jit(solution)/shard_map/all_gather | solution.py:68
  64.7 317.5 %reduce-scatter.10.cloned.1.call-start = ((), (), s32[]{:S(2)}) async-start(), calls=%async_computation.9 | async-start | bytes 2228224
  245.7 218.0 %all-gather.10.cloned.1.call-start = ((), (), s32[]{:S(2)}) async-start(), calls=%async_computation.5 | async-start | bytes 1081344 | tf_op jit(solution)/shard_map/all_gather | solution.py:69
  246.3 441.5 %reduce-scatter.14.cloned.1.call-start = ((), (), s32[]{:S(2)}) async-start(), calls=%async_computation.11 | async-start | bytes 2162688
  372.4 5.3 copy-start.28
  373.7 11.7 copy-start.5
  378.2 9.8 copy-start.23
  394.1 415.5 %all-reduce.4.cloned.1.call-start = ((), (), s32[]{:S(2)}) async-start(), calls=%async_computation.7 | async-start | bytes 1048576 | tf_op jit(solution)/shard_map/psum | solution.py:84
  449.2 17.5 %copy-start.3 = (f32[128,512]{1,0:T(8,128)}, f32[128,512]{1,0:T(8,128)S(1)}, u32[]{:S(2)}) copy-start(f32[128,512]{1,0:T(8,128)S(1)} %fusion.75) | copy-start | bytes 786436
  449.2 5.7 copy-start.30
  449.2 14.4 %copy-start.25 = (f32[32,512]{1,0:T(8,128)S(1)}, f32[32,512]{1,0:T(8,128)}, u32[]{:S(2)}) copy-start(f32[32,512]{1,0:T(8,128)} %copy-done.24) | copy-start | bytes 196612
  452.0 14.8 %copy-start.10 = (f32[128,512]{1,0:T(8,128)}, f32[128,512]{1,0:T(8,128)S(1)}, u32[]{:S(2)}) copy-start(f32[128,512]{1,0:T(8,128)S(1)} %fusion.73) | copy-start | bytes 786436
  454.9 234.7 %copy-start.15 = (f32[128,512]{1,0:T(8,128)}, f32[128,512]{1,0:T(8,128)S(1)}, u32[]{:S(2)}) copy-start(f32[128,512]{1,0:T(8,128)S(1)} %fusion.72) | copy-start | bytes 786436
  689.6 393.3 %copy-start.26 = (f32[32,512]{1,0:T(8,128)S(1)}, f32[32,512]{1,0:T(8,128)}, u32[]{:S(2)}) copy-start(f32[32,512]{1,0:T(8,128)} %copy-done.24) | copy-start | bytes 196612
  689.6 339.2 %reduce-scatter.12.cloned.1.call-start = ((), (), s32[]{:S(2)}) async-start(), calls=%async_computation.10 | async-start | bytes 1081344
  691.7 424.2 %copy-start.1 = (f32[2,512,512]{2,1,0:T(8,128)S(1)}, f32[2,512,512]{2,1,0:T(8,128)}, u32[]{:S(2)}) copy-start(f32[2,512,512]{2,1,0:T(8,128)} %all-gather.8.cloned.1.call-done) | copy-start | bytes 6291460
  691.7 424.2 %all-gather.14.cloned.1.call-start = ((), (), s32[]{:S(2)}) async-start(), calls=%async_computation.8 | async-start | bytes 2162688 | tf_op jit(solution)/shard_map/all_gather | solution.py:85
  811.5 386.2 %all-gather.12.cloned.1.call-start = ((), (), s32[]{:S(2)}) async-start(), calls=%async_computation.6 | async-start | bytes 1081344 | tf_op jit(solution)/shard_map/all_gather | solution.py:110
  1083.6 39.2 %copy-start.6 = (f32[128,512]{1,0:T(8,128)S(1)}, f32[128,512]{1,0:T(8,128)}, u32[]{:S(2)}) copy-start(f32[128,512]{1,0:T(8,128)} %copy-done.5) | copy-start | bytes 786436
  1083.6 39.2 %copy-start.13 = (f32[128,512]{1,0:T(8,128)S(1)}, f32[128,512]{1,0:T(8,128)}, u32[]{:S(2)}) copy-start(f32[128,512]{1,0:T(8,128)} %copy-done.12) | copy-start | bytes 786436
  1083.6 39.2 %copy-start.18 = (f32[128,512]{1,0:T(8,128)S(1)}, f32[128,512]{1,0:T(8,128)}, u32[]{:S(2)}) copy-start(f32[128,512]{1,0:T(8,128)} %copy-done.17) | copy-start | bytes 786436
  1083.6 39.2 %copy-start.21 = (f32[128,512]{1,0:T(8,128)S(1)}, f32[128,512]{1,0:T(8,128)}, u32[]{:S(2)}) copy-start(f32[128,512]{1,0:T(8,128)} %fusion.76) | copy-start | bytes 786436
  (20 other events, 41.6 us)
Sparse Core Ops, SparseCore 0:
  10.1 49.0 all-gather.5
  64.1 170.3 all-reduce.5
  238.1 79.5 all-gather.7
  320.6 61.5 reduce-scatter.9
  385.7 77.9 all-gather.9
  468.6 219.1 reduce-scatter.13
  690.1 119.5 all-reduce.3
  814.7 214.1 reduce-scatter.11
  1032.5 83.3 all-gather.13
  1119.4 78.2 all-gather.11
where the time goes:
time: 1230 us; the launch traced here: 1220 us
  waiting for transfers between devices  953 us (77%)
  other arithmetic  86.7 us (7%)
  matrix products  60 us (5%)
  blocking collectives  52.4 us (4%)
  local copies, waits for them, and re-layouts  49.1 us (4%)
  between operations  15.1 us (1%)
    unnamed x13, waiting for transfers between devices  441 us
    psum x1, waiting for transfers between devices, broadcast(): return lax.psum(kept, axis)  170 us
    psum x1, waiting for transfers between devices, per_device(): panel_part = lax.psum(panel_part, 'col')  118 us
    another operation x4, other arithmetic, lower_inverse(): lax.linalg.triangular_solve(factor, identity, left_side=True, lower=True)  82.5 us
    all_gather x1, waiting for transfers between devices, per_device(): lax.all_gather(diag_factor, 'row', axis=1, tiled=True)  68 us
    all_gather x1, waiting for transfers between devices, per_device(): corner_total = lax.all_gather(corner_part, 'row', axis=0, tiled=True)  64.2 us
    psum x1, blocking collectives, per_device(): corner_part = lax.psum(corner_part, 'col')  52.4 us
    all_gather x1, waiting for transfers between devices, per_device(): row_band = lax.all_gather(factor_rows, 'col', axis=0, tiled=True)  51.3 us
  transfers between devices with their start and end apart: 10, of which 10 were waited for; matrix products, arithmetic and copies ran while one was open for 14% of the time, Pallas kernels for 0%

commit v1 on v0

v1 whole, which is shorter than its diff:
```python
import functools

import jax
import jax.numpy as jnp
from jax import lax
from jax.experimental import pallas as pl
from jax.experimental.pallas import tpu as pltpu
from jax.sharding import PartitionSpec as P

MESH = pl.DeviceIdType.MESH
F32 = jnp.float32
BF16 = jnp.bfloat16
NX, NY, NZ = 4, 8, 8
CHIPS_RING = NZ
NG = 2
B = 512
W = B // NG
ROWS = 32
ORDER = (0, -1, 1, -2, 2, -3, 3, -4)


def split(a):
    hi = a.astype(BF16)
    return hi, (a - hi.astype(F32)).astype(BF16)


def dot(a, b):
    return jnp.dot(a, b, preferred_element_type=F32)


def mm_split(a, b):
    return dot(a[0], b[0]) + (dot(a[0], b[1]) + dot(a[1], b[0]))


def mm(a, b):
    return mm_split(split(a), split(b))


def gather_kernel(
    t_ref, r_ref, f_ref, g_ref, x_ref,
    tbuf, thi, tlo, band, rbuf, psum, sbuf, fbuf, xr, xo, xst, xs, xs2, gm, gy, sg, gx, gz, gsib,
    sib_s, sib_r, loc, zs, zr, ys, xsm, rr, ss, sr, as_, ar, gys, gyr, gxs, gxr, gas, gar, gzs, gzr,
):
    row = lax.axis_index("row")
    col = lax.axis_index("col")
    y, x = row // NX, lax.rem(row, NX)
    z, k = col // 2, lax.rem(col, 2)

    def dev(px, py, pz, pk):
        return {"row": py * NX + px, "col": pz * 2 + pk}

    def up(v, s, n):
        return lax.rem(v + (s + n), n)

    sib = dev(x, y, z, 1 - k)
    zpeer = [dev(x, y, up(z, s, NZ), k) for s in range(1, NZ)]
    ypeer = [dev(x, up(y, s, NY), z, k) for s in range(1, NY)]
    xpeer = [dev(up(x, s, NX), y, z, k) for s in range(1, NX)]
    zup, zdn = zpeer[0], zpeer[-1]
    yup, ydn = ypeer[0], ypeer[-1]
    xup, xdn = xpeer[0], xpeer[-1]
    d = up(y - z, NY, NY)

    barrier = pltpu.get_barrier_semaphore()
    partners = [sib] + zpeer + ypeer + xpeer
    for p in partners:
        pl.semaphore_signal(barrier, inc=1, device_id=p, device_id_type=MESH)
    pl.semaphore_wait(barrier, len(partners))

    sends = []

    def put(src, dst, ssem, rsem, target, cond=None):
        c = pltpu.make_async_remote_copy(
            src_ref=src, dst_ref=dst, send_sem=ssem, recv_sem=rsem, device_id=target, device_id_type=MESH
        )
        if cond is None:
            c.start()
        else:
            pl.when(cond)(c.start)
        sends.append((c, cond))

    def got(ref, sem):
        pltpu.make_async_remote_copy(
            src_ref=ref, dst_ref=ref, send_sem=sem, recv_sem=sem, device_id=sib, device_id_type=MESH
        ).wait_recv()

    for g in range(NG):
        put(r_ref.at[1 - k, g], band.at[g, z, k], sib_s.at[g], sib_r.at[g], sib)
    for g in range(NG):
        band[g, z, k] = r_ref[k, g]
    put(t_ref, tbuf.at[k], sib_s.at[NG], sib_r.at[NG], sib)
    tcopy = pltpu.make_async_copy(t_ref, tbuf.at[k], loc.at[0])
    tcopy.start()
    put(f_ref.at[1 - k], fbuf.at[k], sib_s.at[NG + 1], sib_r.at[NG + 1], sib)
    fbuf[k] = f_ref[k]

    steps = [(g, j) for g in range(NG) for j in range(NZ)]
    lb, ld, le = 4, 5, 6
    own_copies = []

    def stage_a(i):
        g, j = steps[i]
        zz = up(z, ORDER[j], NZ)
        if j == 0:
            got(band.at[g, z, 1 - k], sib_r.at[g])
            put(band.at[g, z], band.at[g, z], zs.at[0, g, 0], zr.at[g, z], zup)
            put(band.at[g, z], band.at[g, z], zs.at[1, g, 0], zr.at[g, z], zdn)
        else:
            got(band.at[g, zz], zr.at[g, zz])
            hop = abs(ORDER[j])
            if ORDER[j] < 0 and hop < NZ // 2:
                put(band.at[g, zz], band.at[g, zz], zs.at[0, g, hop], zr.at[g, zz], zup)
            if ORDER[j] > 0 and hop < NZ // 2 - 1:
                put(band.at[g, zz], band.at[g, zz], zs.at[1, g, hop], zr.at[g, zz], zdn)
        src = d == 0
        put(band.at[g, zz], rbuf.at[g, x, zz], ys.at[0, g, j], rr.at[g, x, zz], yup, src)
        put(band.at[g, zz], rbuf.at[g, x, zz], ys.at[1, g, j], rr.at[g, x, zz], ydn, src)

        @pl.when(src)
        def _():
            rbuf[g, x, zz] = band[g, zz]

    def stage_b(i):
        g, j = steps[i]
        zz = up(z, ORDER[j], NZ)
        slot, sem = rbuf.at[g, x, zz], rr.at[g, x, zz]

        @pl.when(d != 0)
        def _():
            got(slot, sem)

        put(slot, slot, ys.at[0, g, j], sem, yup, jnp.logical_and(d >= 1, d <= 3))
        put(slot, slot, ys.at[1, g, j], sem, ydn, d >= 6)
        put(slot, slot, xsm.at[0, g, j], sem, xup)
        put(slot, slot, xsm.at[1, g, j], sem, xdn)

    def stage_d(i):
        g, j = steps[i]
        zz = up(z, ORDER[j], NZ)
        left, right = up(x, -1, NX), up(x, 1, NX)
        got(rbuf.at[g, left, zz], rr.at[g, left, zz])
        got(rbuf.at[g, right, zz], rr.at[g, right, zz])
        origin, target = (left, xup) if j % 2 == 0 else (right, xdn)
        put(rbuf.at[g, origin, zz], rbuf.at[g, origin, zz], xsm.at[2, g, j], rr.at[g, origin, zz], target)

    def stage_e(i):
        g, j = steps[i]
        zz = up(z, ORDER[j], NZ)
        far = up(x, 2, NX)
        got(rbuf.at[g, far, zz], rr.at[g, far, zz])

    def piece(g, xx):
        b = split(rbuf[g, xx].reshape(NZ * 2 * ROWS, W))
        lanes = slice(512 * (xx % 2), 512 * (xx % 2) + 512)
        a = (thi[xx // 2, :, lanes], tlo[xx // 2, :, lanes])
        part = mm_split(a, b).reshape(NZ, 2 * ROWS, W)
        if xx == 0:
            psum[g] = part
        else:
            psum[g] += part

    def scatter(g):
        for s in range(1, NZ):
            to = up(z, s, NZ)
            put(psum.at[g, to], sbuf.at[g, z], ss.at[g, s], sr.at[g, z], zpeer[s - 1])
        sbuf[g, z] = psum[g, z]

    n = len(steps)
    work = []
    for i in range(n + le):
        if i < n:
            stage_a(i)
        if 0 <= i - lb < n:
            stage_b(i - lb)
        if 0 <= i - ld < n:
            stage_d(i - ld)
        if 0 <= i - le < n:
            stage_e(i - le)
            g, j = steps[i - le]
            if work:
                work.pop(0)()
            if j == NZ - 1:
                if g == 0:
                    tcopy.wait()
                    got(tbuf.at[1 - k], sib_r.at[NG])
                    for h in range(2):
                        thi[h], tlo[h] = split(tbuf[h])
                for xx in range(NX):
                    work.append(functools.partial(piece, g, xx))
                work.append(functools.partial(scatter, g))
    for item in work:
        item()

    got(fbuf.at[1 - k], sib_r.at[NG + 1])
    for g in range(NG):
        for s in range(1, NZ):
            frm = up(z, s, NZ)
            got(sbuf.at[g, frm], sr.at[g, frm])
        total = sbuf[g, 0]
        for s in range(1, NZ):
            total = total + sbuf[g, s]
        lanes = slice(g * W, g * W + W)
        xr[:, :, lanes] = fbuf[:, :, lanes] - 2.0 * total.reshape(2, ROWS, W)

    put(xr.at[1 - k], xo.at[k], sib_s.at[NG + 2], sib_r.at[NG + 2], sib)
    xo[k] = xr[k]
    xall = xr[...].reshape(2 * ROWS, B)
    for s in range(NZ):
        xst[s] = xall[:, 64 * s : 64 * s + 64]
    for s in range(1, NZ):
        to = up(z, s, NZ)
        put(xst.at[to], xs.at[z], as_.at[s], ar.at[z], zpeer[s - 1])
    xs[z] = xst[z]
    for s in range(1, NZ):
        frm = up(z, s, NZ)
        got(xs.at[frm], ar.at[frm])
    first = k == 0
    put(xs, xs2, sib_s.at[NG + 3], sib_r.at[NG + 3], sib, k == 1)

    def gram(b, src):
        a = split(src[...].reshape(NZ * 64, 64).T)
        for g in range(NG):
            bb = split(band[g].reshape(NZ * 64, W))
            gm[b, :, :, g * W : g * W + W] = mm_split(a, bb).reshape(NY, 8, W)

    def plane_reduce_start(b, cond):
        for s in range(1, NY):
            to = up(y, s, NY)
            put(gm.at[b, to], gy.at[b, y], gys.at[b, s], gyr.at[b, y], ypeer[s - 1], cond)

    gram(0, xs)
    plane_reduce_start(0, None)

    @pl.when(first)
    def _():
        got(xs2, sib_r.at[NG + 3])
        gram(1, xs2)

    plane_reduce_start(1, first)
    conds = (None, first)

    def when(cond, fn):
        if cond is None:
            fn()
        else:
            pl.when(cond)(fn)

    def y_sum(b):
        gy[b, y] = gm[b, y]
        for s in range(1, NY):
            frm = up(y, s, NY)
            got(gy.at[b, frm], gyr.at[b, frm])
        total = gy[b, 0]
        for s in range(1, NY):
            total = total + gy[b, s]
        sg[b] = total
        gx[b, x] = total

    def x_sum(b):
        for s in range(1, NX):
            frm = up(x, s, NX)
            got(gx.at[b, frm], gxr.at[b, frm])
        gz[b, z, y] = (gx[b, 0] + gx[b, 1]) + (gx[b, 2] + gx[b, 3])

    def y_wait(b):
        for s in range(1, NY):
            frm = up(y, s, NY)
            got(gz.at[b, z, frm], gar.at[b, frm])

    for b in range(2):
        when(conds[b], functools.partial(y_sum, b))
        for s in range(1, NX):
            put(sg.at[b], gx.at[b, x], gxs.at[b, s], gxr.at[b, x], xpeer[s - 1], conds[b])
    for b in range(2):
        when(conds[b], functools.partial(x_sum, b))
        for s in range(1, NY):
            put(gz.at[b, z, y], gz.at[b, z, y], gas.at[b, s], gar.at[b, y], ypeer[s - 1], conds[b])
    for j in range(NZ):
        zz = up(z, ORDER[j], NZ)
        hop = abs(ORDER[j])
        for b in range(2):
            if j == 0:
                when(conds[b], functools.partial(y_wait, b))
            else:
                when(conds[b], functools.partial(got, gz.at[b, zz], gzr.at[b, zz]))
            if j == 0 or (ORDER[j] < 0 and hop < NZ // 2):
                put(gz.at[b, zz], gz.at[b, zz], gzs.at[0, b, hop], gzr.at[b, zz], zup, conds[b])
            if j == 0 or (ORDER[j] > 0 and hop < NZ // 2 - 1):
                put(gz.at[b, zz], gz.at[b, zz], gzs.at[1, b, hop], gzr.at[b, zz], zdn, conds[b])
    put(gz.at[0], gsib.at[0], sib_s.at[NG + 4], sib_r.at[NG + 4], sib)
    put(gz.at[1], gsib.at[1], sib_s.at[NG + 5], sib_r.at[NG + 5], sib, first)

    got(xo.at[1 - k], sib_r.at[NG + 2])
    x_ref[...] = xo[...]
    got(gsib.at[0], sib_r.at[NG + 4])

    @pl.when(first)
    def _():
        g_ref[0] = gz[0].reshape(B, B)
        g_ref[1] = gz[1].reshape(B, B)
        g_ref[2] = gsib[0].reshape(B, B)

    @pl.when(k == 1)
    def _():
        got(gsib.at[1], sib_r.at[NG + 5])
        g_ref[0] = gsib[0].reshape(B, B)
        g_ref[1] = gsib[1].reshape(B, B)
        g_ref[2] = gz[0].reshape(B, B)

    for c, cond in sends:
        if cond is None:
            c.wait_send()
        else:
            pl.when(cond)(c.wait_send)


def gather_call(trailing, rows4, grads4):
    dma = pltpu.SemaphoreType.DMA
    vm = pl.BlockSpec(memory_space=pltpu.VMEM)
    return pl.pallas_call(
        gather_kernel,
        out_shape=(
            jax.ShapeDtypeStruct((3, B, B), F32),
            jax.ShapeDtypeStruct((2, ROWS, B), F32),
        ),
        in_specs=[pl.BlockSpec(memory_space=pl.ANY), vm, vm],
        out_specs=(vm, vm),
        scratch_shapes=[
            pltpu.VMEM((2, 512, 1024), F32),
            pltpu.VMEM((2, 512, 1024), BF16),
            pltpu.VMEM((2, 512, 1024), BF16),
            pltpu.VMEM((NG, NZ, 2, ROWS, W), F32),
            pltpu.VMEM((NG, NX, NZ, 2, ROWS, W), F32),
            pltpu.VMEM((NG, NZ, 2 * ROWS, W), F32),
            pltpu.VMEM((NG, NZ, 2 * ROWS, W), F32),
            pltpu.VMEM((2, ROWS, B), F32),
            pltpu.VMEM((2, ROWS, B), F32),
            pltpu.VMEM((2, ROWS, B), F32),
            pltpu.VMEM((NZ, 64, 64), F32),
            pltpu.VMEM((NZ, 64, 64), F32),
            pltpu.VMEM((NZ, 64, 64), F32),
            pltpu.VMEM((2, NY, 8, B), F32),
            pltpu.VMEM((2, NY, 8, B), F32),
            pltpu.VMEM((2, 8, B), F32),
            pltpu.VMEM((2, NX, 8, B), F32),
            pltpu.VMEM((2, NZ, NY, 8, B), F32),
            pltpu.VMEM((2, NZ, NY, 8, B), F32),
            dma((NG + 6,)), dma((NG + 6,)), dma((1,)),
            dma((2, NG, NZ // 2)), dma((NG, NZ)),
            dma((2, NG, NZ)), dma((3, NG, NZ)), dma((NG, NX, NZ)),
            dma((NG, NZ)), dma((NG, NZ)),
            dma((NZ,)), dma((NZ,)),
            dma((2, NY)), dma((2, NY)),
            dma((2, NX)), dma((2, NX)),
            dma((2, NY)), dma((2, NY)),
            dma((2, 2, NZ // 2)), dma((2, NZ)),
        ],
        compiler_params=pltpu.CompilerParams(
            collective_id=0, has_side_effects=True, vmem_limit_bytes=48 * 1024 * 1024
        ),
        name="panel_gather_and_gram",
    )(trailing, rows4, grads4)


def invert(lower, out_ref):
    n = 128
    r = lax.broadcasted_iota(jnp.int32, (n, n), 0)
    c = lax.broadcasted_iota(jnp.int32, (n, n), 1)
    blocks = [lower(q, q) for q in range(4)]
    inv = []
    for a in blocks:
        diag = jnp.sum(jnp.where(r == c, a, 0.0), axis=1, keepdims=True)
        inv.append(jnp.where(r == c, 1.0 / diag, 0.0))
    for lb in range(7):
        mask = ((r >> (lb + 1)) == (c >> (lb + 1))) & ((r >> lb) > (c >> lb))
        for q in range(4):
            cut = jnp.where(mask, blocks[q], 0.0)
            yy = split(inv[q])
            inv[q] = inv[q] - mm_split(yy, split(mm_split(split(cut), yy)))
    zero = jnp.zeros((n, n), F32)
    wide = []
    for h in range(2):
        a, b = inv[2 * h], inv[2 * h + 1]
        low = -mm(b, mm(lower(2 * h + 1, 2 * h), a))
        wide.append(jnp.concatenate([jnp.concatenate([a, zero], 1), jnp.concatenate([low, b], 1)], 0))
    corner = jnp.concatenate(
        [jnp.concatenate([lower(2, 0), lower(2, 1)], 1), jnp.concatenate([lower(3, 0), lower(3, 1)], 1)], 0
    )
    low = -mm(wide[1], mm(corner, wide[0]))
    out_ref[0:256, 0:256] = wide[0]
    out_ref[0:256, 256:512] = jnp.zeros((256, 256), F32)
    out_ref[256:512, 0:256] = low
    out_ref[256:512, 256:512] = wide[1]


def chain_kernel(full_ref, g_ref, x_ref, h_ref, b_ref, c_ref, v1, v2, v1t, e_ref, m_ref, w1, w2):
    def part(p):
        return full_ref[:, p * B : p * B + B]

    def tile(p):
        return lambda i, j: full_ref[128 * i : 128 * i + 128, p * B + 128 * j : p * B + 128 * j + 128]

    r = lax.broadcasted_iota(jnp.int32, (B, B), 0)
    c = lax.broadcasted_iota(jnp.int32, (B, B), 1)

    def lowered(p):
        return jnp.where(r > c, p, jnp.where(r == c, 0.5 * p, 0.0))

    invert(tile(0), v1)
    invert(tile(1), v2)
    v1t[...] = v1[...].T
    v2t = split(v2[...].T)
    vs1 = split(v1[...])
    vs2 = split(v2[...])
    l21 = split(part(2))
    m_ref[...] = mm_split(l21, vs1)
    ms = split(m_ref[...])
    h2 = mm_split(split(x_ref[1]), vs2)
    h_ref[:, B : 2 * B] = h2
    h_ref[:, 0:B] = mm_split(split(x_ref[0]), vs1) - mm_split(split(h2), ms)
    hr2 = mm_split(v2t, split(g_ref[2]))
    hr1 = mm_split(v2t, split(g_ref[1]))
    p2 = part(4) - hr2
    q2 = lowered(mm_split(split(part(1).T), split(jnp.where(r >= c, p2, 0.0))))
    w1[...] = mm_split(split(q2 + q2.T), vs2)
    w2[...] = 0.5 * mm_split(v2t, split(w1[...]))
    p1 = part(3) - hr1
    coupling = mm_split(split(p1), vs1) - 2.0 * mm_split(split(w2[...]), ms)
    e_ref[...] = coupling
    corner = part(5) - mm_split(split(v1t[...]), split(g_ref[0])) + mm_split(split(m_ref[...].T), split(hr1))
    grad = jnp.where(r >= c, corner - mm_split(split(coupling.T), l21), 0.0)
    q1 = lowered(mm_split(split(part(0).T), split(grad)))
    w1[...] = q1 + q1.T
    own = pl.ds(pl.multiple_of(lax.axis_index("row") * 16, 16), 16)
    b_ref[1] = w2[own, :]
    c_ref[...] = e_ref[own, :]
    b_ref[0] = 0.5 * mm(mm(v1t[own, :], w1[...]), v1[...])


def chain_call(full, grams, xrows):
    vm = pl.BlockSpec(memory_space=pltpu.VMEM)
    square = pltpu.VMEM((B, B), F32)
    return pl.pallas_call(
        chain_kernel,
        out_shape=(
            jax.ShapeDtypeStruct((ROWS, 2 * B), F32),
            jax.ShapeDtypeStruct((2, 16, B), F32),
            jax.ShapeDtypeStruct((16, B), F32),
        ),
        in_specs=[vm, vm, vm],
        out_specs=(vm, vm, vm),
        scratch_shapes=[square] * 7,
        compiler_params=pltpu.CompilerParams(vmem_limit_bytes=48 * 1024 * 1024),
        name="small_block_chain",
    )(full, grams, xrows)


def per_device(
    trailing_grad, factor_rows, factor_grad, diag_factor, cross_factor, cross_grad, corner_grad
):
    col_place = lax.axis_index("col")
    cross_wide = lax.all_gather(cross_grad, "col", axis=1, tiled=True)
    corner_wide = lax.all_gather(corner_grad, "col", axis=1, tiled=True)
    small = jnp.concatenate([diag_factor[0], diag_factor[1], cross_factor, cross_wide, corner_wide], 1)
    full = lax.all_gather(small, "row", axis=0, tiled=True)
    rows4 = factor_rows.reshape(ROWS, 2, NG, W).transpose(1, 2, 0, 3)
    grads4 = factor_grad.reshape(ROWS, 2, B).transpose(1, 0, 2)
    grams, xrows = gather_call(trailing_grad, rows4, grads4)
    rows_grad, blocks, coupling = chain_call(full, grams, xrows)
    corner_cols = corner_grad.shape[1]
    blocks_grad = lax.dynamic_slice(blocks, (0, 0, col_place * corner_cols), (2, 16, corner_cols))
    coupling_grad = lax.dynamic_slice(coupling, (0, col_place * corner_cols), (16, corner_cols))
    return (rows_grad, blocks_grad, coupling_grad)


def solution(mesh):
    return jax.shard_map(
        per_device,
        mesh=mesh,
        in_specs=(
            P("row", "col"),
            P(("row", "col"), None),
            P(("row", "col"), None),
            P(None, "row", None),
            P("row", None),
            P("row", "col"),
            P("row", "col"),
        ),
        out_specs=(P(("row", "col"), None), P(None, "row", "col"), P("row", "col")),
        check_vma=False,
    )
```

time: 1230 us -> 241 us (0.20)
  waiting for transfers between devices: 953 us -> 0.04 us
  Pallas kernels: 0 us -> 178 us
  other arithmetic: 86.7 us -> 0 us
  matrix products: 60 us -> 0 us
  local copies, waits for them, and re-layouts: 49.1 us -> 8.18 us
    unnamed x13 -> x1, waiting for transfers between devices: 441 us -> 0.02 us
    psum x2 -> x0, waiting for transfers between devices: 288 us -> none  [the longest x1 170 us: broadcast(): return lax.psum(kept, axis)]
    all_gather x5 -> x1, waiting for transfers between devices: 225 us -> 0.02 us  [per_device(): full = lax.all_gather(small, 'row', axis=0, tiled=True)]
    pallas_call x0 -> x2, Pallas kernels: none -> 178 us  [the longest x1 157 us: gather_call(): pl.pallas_call(gather_kernel, out_shape=(jax.ShapeDtypeStruct((3, B, B),...]
    another operation x6 -> x0, other arithmetic: 85.9 us -> none  [the longest x4 82.5 us: lower_inverse(): lax.linalg.triangular_solve(factor, identity, left_side=True, lower=True)]
    psum x1 -> x0, blocking collectives: 52.4 us -> none  [per_device(): corner_part = lax.psum(corner_part, 'col')]
    dot_general x15 -> x0, matrix products: 43.8 us -> none  [the longest x7 18.7 us: inner_t(): lax.dot_general(left, right, (((0,), (0,)), ((), ())), precision=highest,...]
    all_gather x0 -> x2, blocking collectives: none -> 40.1 us  [the longest x1 25.1 us: per_device(): cross_wide = lax.all_gather(cross_grad, 'col', axis=1, tiled=True)]
  transfers between devices with their start and end apart: 10 -> 1, of which waited for: 10 -> 0; matrix products, arithmetic and copies ran while one was open for 14% -> 1% of each run, Pallas kernels for 0% -> 65%
where the time goes in v1:
time: 241 us; the launch traced here: 240 us
  Pallas kernels  178 us (74%)
  blocking collectives  40.1 us (17%)
  between operations  14.1 us (6%)
  local copies, waits for them, and re-layouts  8.18 us (3%)
    pallas_call x1, Pallas kernels, gather_call(): pl.pallas_call(gather_kernel, out_shape=(jax.ShapeDtypeStruct((3, B, B),...  157 us
    all_gather x1, blocking collectives, per_device(): cross_wide = lax.all_gather(cross_grad, 'col', axis=1, tiled=True)  25.1 us
    pallas_call x1, Pallas kernels, chain_call(): pl.pallas_call(chain_kernel, out_shape=(jax.ShapeDtypeStruct((ROWS, 2 * B...  20.8 us
    all_gather x1, blocking collectives, per_device(): corner_wide = lax.all_gather(corner_grad, 'col', axis=1, tiled=True)  15.1 us
  transfers between devices with their start and end apart: 1, of which 0 were waited for; matrix products, arithmetic and copies ran while one was open for 1% of the time, Pallas kernels for 65%

profile of v1, /device:TPU:1, one launch (start us, length us, event | category | flops | bytes accessed | tf_op | source)
XLA Modules:
  0.0 240.3 jit_solution(4538955987169332172)
XLA Ops:
  7.2 0.0 all-gather.4.cloned.1.call-start
  7.2 0.8 bitcast_dynamic-update-slice_fusion.3
  8.0 0.8 bitcast_dynamic-update-slice_fusion.2
  8.7 25.1 %all-gather = f32[16,64,16]{1,2,0:T(8,128)S(1)} all-gather(f32[1,64,16]{1,2,0:T(8,128)} %bitcast.31), channel_id=1, replica_groups=mesh['row'=32,'col'=16] {'col'}, dimensions={0}, use_global_device_ids=true | all-gather | bytes 69632 | tf_op jit(solution)/shard_map/all_gather | solution.py:462
  33.9 0.1 reshape.15
  34.0 15.1 %all-gather.1 = f32[16,32,16]{1,2,0:T(8,128)S(1)} all-gather(f32[1,32,16]{1,2,0:T(8,128)} %bitcast.32), channel_id=1, replica_groups=mesh['row'=32,'col'=16] {'col'}, dimensions={0}, use_global_device_ids=true | all-gather | bytes 34816 | tf_op jit(solution)/shard_map/all_gather | solution.py:463
  49.1 0.1 reshape.17
  49.2 0.8 constant_dynamic-update-slice_fusion
  49.9 0.0 copy-start.1
  50.0 0.7 copy-done.1
  50.6 0.0 all-gather.4.cloned.1.call-update
  50.7 1.0 reshape.12
  51.7 0.9 copy.23
  52.6 0.0 copy-start
  52.6 1.6 copy-done
  54.2 157.1 %panel_gather_and_gram.1 = (f32[3,512,512]{2,1,0:T(8,128)S(1)}, f32[2,32,512]{2,1,0:T(8,128)S(1)}) custom-call(f32[512,1024]{1,0:T(8,128)S(1)} %copy-done, f32[2,2,32,256]{3,2,1,0:T(8,128)S(1)} %bitcast.28, f32[2,32,512]{2,1,0:T(8,128)S(1)} %bitcast.29), custom_call_target="tpu_custom_call" | custom-call | tf_op jit(solution)/shard_map/panel_gather_and_gram/pallas_call | solution.py:320
  211.3 0.0 all-gather.4.cloned.1.call-done.full_ref
  211.3 20.8 %small_block_chain.1 = (f32[32,1024]{1,0:T(8,128)}, f32[2,16,512]{2,1,0:T(8,128)S(1)}, f32[16,512]{1,0:T(8,128)S(1)}) custom-call(f32[512,3072]{1,0:T(8,128)} %all-gather.4.cloned.1.call-done.full_ref, f32[3,512,512]{2,1,0:T(8,128)S(1)} %get-tuple-element.8.g_ref, f32[2,32,512]{2,1,0:T(8,128)S(1)} %get-tuple-element.9.x_ref), custom_call_target="tpu_custom_call" | custom-call | tf_op jit(solution)/shard_map/small_block_chain/pallas_call | solution.py:443
  232.1 0.7 constant_dynamic-slice_fusion.1
  232.8 0.7 constant_dynamic-slice_fusion
  (5 shorter events, 0.1 us)
Async XLA Ops:
  7.2 204.2 %all-gather.4.cloned.1.call-start = ((), (), s32[]{:S(2)}) async-start(), calls=%async_computation | async-start | bytes 6488064 | tf_op jit(solution)/shard_map/all_gather | solution.py:465
  49.9 0.7 copy-start.1
  52.6 1.6 copy-start
Sparse Core Ops, SparseCore 0:
  50.8 101.2 all-gather.3

commit v2 on v1

v2 whole, which is shorter than its diff:
```python
import functools

import jax
import jax.numpy as jnp
from jax import lax
from jax.experimental import pallas as pl
from jax.experimental.pallas import tpu as pltpu
from jax.sharding import PartitionSpec as P

MESH = pl.DeviceIdType.MESH
F32 = jnp.float32
BF16 = jnp.bfloat16
NX, NY, NZ = 4, 8, 8
NG = 2
B = 512
W = B // NG
W2 = B // 2
ROWS = 32
ORDER = (0, -1, 1, -2, 2, -3, 3, -4)
STEPS = sorted(((g, o) for g in range(NG) for o in ORDER), key=lambda s: (abs(s[1]) + 2 * s[0], s[0]))
STEP_COUNT = len(STEPS)
LAST0 = max(i for i, s in enumerate(STEPS) if s[0] == 0)


def pick(values, n):
    words = [sum(v << (4 * i) for i, v in enumerate(values[h : h + 8])) for h in (0, 8)]
    return (jnp.where(n < 8, words[0], words[1]) >> (4 * lax.rem(n, 8))) & 7


def split(a):
    hi = a.astype(BF16)
    return hi, (a - hi.astype(F32)).astype(BF16)


def dot(a, b):
    return jnp.dot(a, b, preferred_element_type=F32)


def mm_split(a, b):
    return dot(a[0], b[0]) + (dot(a[0], b[1]) + dot(a[1], b[0]))


def mm(a, b):
    return mm_split(split(a), split(b))


def panel_kernel(
    t_ref, r_ref, f_ref, diag_ref, cross_ref, cg_ref, co_ref,
    rows_ref, b_ref, c_ref,
    tbuf, thi, tlo, band, rbuf, psum, sbuf, fbuf, xr, xo, xst, xs, xs2, gm, gy, sg, gx, gz,
    lloc, cgl, col_, lbuf, cgb, ltr, fold, v1, v2, v1t, v2t, mmat, mt, w1, w2, sbm, cpl, outp,
    sib_s, sib_r, loc, zs, zr, ys, xsm, rr, ss, sr, as_, ar, gys, gyr, gxs, gxr, gas, gar, gbs, gbr, gzs, gzr,
    gws, gwr, lxs, lxr, lys, lyr, lzs, lzr, lfs, lfr, cs_, cr,
):
    local = [
        pltpu.make_async_copy(diag_ref, lloc.at[pl.ds(0, 2)], loc.at[1]),
        pltpu.make_async_copy(cross_ref, lloc.at[2], loc.at[2]),
        pltpu.make_async_copy(cg_ref, cgl, loc.at[3]),
        pltpu.make_async_copy(co_ref, col_, loc.at[4]),
    ]
    for c in local:
        c.start()
    row = lax.axis_index("row")
    col = lax.axis_index("col")
    y, x = row // NX, lax.rem(row, NX)
    z, k = col // 2, lax.rem(col, 2)

    def dev(px, py, pz, pk):
        return {"row": py * NX + px, "col": pz * 2 + pk}

    def up(v, s, n):
        return lax.rem(v + (s + n), n)

    sib = dev(x, y, z, 1 - k)
    zpeer = [dev(x, y, up(z, s, NZ), k) for s in range(1, NZ)]
    ypeer = [dev(x, up(y, s, NY), z, k) for s in range(1, NY)]
    xpeer = [dev(up(x, s, NX), y, z, k) for s in range(1, NX)]
    zup, zdn = zpeer[0], zpeer[-1]
    yup, ydn = ypeer[0], ypeer[-1]
    xup, xdn = xpeer[0], xpeer[-1]
    d = up(y - z, NY, NY)

    barrier = pltpu.get_barrier_semaphore()
    partners = [sib] + zpeer + ypeer + xpeer
    for p in partners:
        pl.semaphore_signal(barrier, inc=1, device_id=p, device_id_type=MESH)
    pl.semaphore_wait(barrier, len(partners))

    sends = []
    mode = ["start"]

    def put(src, dst, ssem, rsem, target, cond=None):
        c = pltpu.make_async_remote_copy(
            src_ref=src, dst_ref=dst, send_sem=ssem, recv_sem=rsem, device_id=target, device_id_type=MESH
        )
        act = c.wait_send if mode[0] == "finish" else c.start
        if cond is None:
            act()
        else:
            pl.when(cond)(act)
        if mode[0] == "start":
            sends.append((c, cond))

    def got(ref, sem):
        if mode[0] != "finish":
            pltpu.make_async_remote_copy(
                src_ref=ref, dst_ref=ref, send_sem=sem, recv_sem=sem, device_id=sib, device_id_type=MESH
            ).wait_recv()

    first = k == 0
    for g in range(NG):
        lanes = pl.ds(pl.multiple_of((1 - k) * B + g * W, 128), W)
        put(r_ref.at[:, lanes], band.at[g, z, k], sib_s.at[g], sib_r.at[g], sib)
    rcopies = []
    for g in range(NG):
        lanes = pl.ds(pl.multiple_of(k * B + g * W, 128), W)
        rcopies.append(pltpu.make_async_copy(r_ref.at[:, lanes], band.at[g, z, k], loc.at[5 + g]))
        rcopies[-1].start()
    put(t_ref, tbuf.at[k], sib_s.at[NG], sib_r.at[NG], sib)
    tcopy = pltpu.make_async_copy(t_ref, tbuf.at[k], loc.at[0])
    tcopy.start()
    put(f_ref.at[:, pl.ds(pl.multiple_of((1 - k) * B, 128), B)], fbuf.at[k], sib_s.at[NG + 1], sib_r.at[NG + 1], sib)
    fcopy = pltpu.make_async_copy(f_ref.at[:, pl.ds(pl.multiple_of(k * B, 128), B)], fbuf.at[k], loc.at[5 + NG])
    fcopy.start()
    for c in local:
        c.wait()
    quarter = lax.rem(z, 4)
    half = pl.ds(3 * k, 3)
    for p in range(4):

        @pl.when(quarter == p)
        def _():
            for q in range(3):
                lbuf[p, y, x, 2 * q : 2 * q + 2] = lloc[q, :, 128 * p : 128 * p + 128].reshape(2, 8, 128)

    for s in range(1, NX):
        put(
            lbuf.at[quarter, y, x, half], lbuf.at[quarter, y, x, half], lxs.at[s], lxr.at[x], xpeer[s - 1]
        )
    cgb[z, k] = jnp.zeros((16, 128), F32)
    cgb[z, k, :, 0:64] = cgl[...]
    cgb[z, k, :, 64:96] = col_[...]
    put(cgb.at[z, k], cgb.at[z, k], sib_s.at[NG + 4], sib_r.at[NG + 4], sib)

    def l_rows():
        for s in range(1, NX):
            frm = up(x, s, NX)
            got(lbuf.at[quarter, y, frm, half], lxr.at[frm])
        for s in range(1, NY):
            put(lbuf.at[quarter, y, :, half], lbuf.at[quarter, y, :, half], lys.at[s], lyr.at[y], ypeer[s - 1])

    def l_planes():
        for s in range(1, NY):
            frm = up(y, s, NY)
            got(lbuf.at[quarter, frm, :, half], lyr.at[frm])
        for i, to in enumerate((zup, zdn)):
            put(lbuf.at[quarter, :, :, half], lbuf.at[quarter, :, :, half], lzs.at[i], lzr.at[i], to)

    def l_far():
        below, above = up(quarter, 3, 4), up(quarter, 1, 4)
        got(lbuf.at[below, :, :, half], lzr.at[0])
        part = lbuf.at[below, pl.ds(0, NY // 2), :, half]
        put(part, part, lfs.at[0], lfr.at[0], zup)
        got(lbuf.at[above, :, :, half], lzr.at[1])
        part = lbuf.at[above, pl.ds(NY // 2, NY // 2), :, half]
        put(part, part, lfs.at[1], lfr.at[1], zdn)

    def l_cores():
        far = up(quarter, 2, 4)
        for i in range(2):
            got(lbuf.at[far, pl.ds(i * NY // 2, NY // 2), :, half], lfr.at[i])
        put(lbuf.at[:, :, :, half], lbuf.at[:, :, :, half], sib_s.at[NG + 5], sib_r.at[NG + 5], sib)

    def adjoint_rows():
        got(cgb.at[z, 1 - k], sib_r.at[NG + 4])
        for s in range(1, NZ):
            put(cgb.at[z], cgb.at[z], cs_.at[s], cr.at[z], zpeer[s - 1])

    hops = jnp.where(d <= NY // 2, d, NY - d)
    lag_b = 2 * hops
    lag_d = lag_b + 2
    lag_e = lag_d + 2
    background = {2: l_rows, 8: l_planes, 10: adjoint_rows, 16: l_far, 20: l_cores}

    def step(n):
        o = pick([st[1] + 4 for st in STEPS], n)
        return pick([st[0] for st in STEPS], n), o, lax.rem(z + o + NZ - 4, NZ)

    def stage_a(n):
        g, o, zz = step(n)
        if mode[0] != "finish":

            @pl.when(o == 4)
            def _():
                pltpu.make_async_copy(band.at[g, z, k], band.at[g, z, k], loc.at[5 + g]).wait()
                got(band.at[g, z, 1 - k], sib_r.at[g])

            @pl.when(o != 4)
            def _():
                got(band.at[g, zz], zr.at[g, zz])

        chunk = band.at[g, zz]
        put(chunk, chunk, zs.at[0, g, o], zr.at[g, zz], zup, jnp.logical_and(o >= 1, o <= 4))
        put(chunk, chunk, zs.at[1, g, o], zr.at[g, zz], zdn, jnp.logical_and(o >= 4, o <= 6))
        put(chunk, rbuf.at[g, x, zz], ys.at[0, g, o], rr.at[g, x, zz], yup, d == 0)
        put(chunk, rbuf.at[g, x, zz], ys.at[1, g, o], rr.at[g, x, zz], ydn, d == 0)
        if mode[0] != "finish":

            @pl.when(d == 0)
            def _():
                rbuf[g, x, zz] = band[g, zz]

    def stage_b(n):
        g, o, zz = step(n)
        slot, sem = rbuf.at[g, x, zz], rr.at[g, x, zz]
        if mode[0] != "finish":

            @pl.when(d != 0)
            def _():
                got(slot, sem)

        put(slot, slot, ys.at[0, g, o], sem, yup, jnp.logical_and(d >= 1, d <= 3))
        put(slot, slot, ys.at[1, g, o], sem, ydn, d >= 6)
        put(slot, slot, xsm.at[0, g, o], sem, xup)
        put(slot, slot, xsm.at[1, g, o], sem, xdn)

    def stage_d(n):
        g, o, zz = step(n)
        left, right = up(x, -1, NX), up(x, 1, NX)
        got(rbuf.at[g, left, zz], rr.at[g, left, zz])
        got(rbuf.at[g, right, zz], rr.at[g, right, zz])
        even = lax.rem(o, 2) == 0
        chunk = rbuf.at[g, left, zz]
        put(chunk, chunk, xsm.at[2, g, o], rr.at[g, left, zz], xup, even)
        chunk = rbuf.at[g, right, zz]
        put(chunk, chunk, xsm.at[2, g, o], rr.at[g, right, zz], xdn, jnp.logical_not(even))

    def stage_e(n):
        g, o, zz = step(n)
        far = up(x, 2, NX)
        got(rbuf.at[g, far, zz], rr.at[g, far, zz])

    def piece(g, xx):
        b = split(rbuf[g, xx].reshape(NZ * 2 * ROWS, W))
        psum[g] += mm_split((thi[xx], tlo[xx]), b).reshape(NZ, 2 * ROWS, W)

    def scatter(g):
        for s in range(1, NZ):
            to = up(z, s, NZ)
            put(psum.at[g, to], sbuf.at[g, z], ss.at[g, s], sr.at[g, z], zpeer[s - 1])
        if mode[0] != "finish":
            sbuf[g, z] = psum[g, z]

    def within(n, fn):
        @pl.when(jnp.logical_and(n >= 0, n < STEP_COUNT))
        def _():
            fn(n)

    def first_group(n):
        @pl.when(n == 0)
        def _():
            tcopy.wait()
            got(tbuf.at[1 - k], sib_r.at[NG])

        @pl.when(jnp.logical_and(n >= 0, n < NX))
        def _():
            lanes = pl.ds(pl.multiple_of(lax.rem(n, 2) * 512, 128), 512)
            thi[n], tlo[n] = split(tbuf[n // 2, :, lanes])
            piece(0, n)

        @pl.when(n == NX)
        def _():
            scatter(0)

    psum[...] = jnp.zeros_like(psum)
    mode[0] = "loop"

    def body(i, carry):
        for at, task in background.items():
            pl.when(i == at)(task)
        within(i, stage_a)
        within(i - lag_b, stage_b)
        within(i - lag_d, stage_d)
        within(i - lag_e, stage_e)
        first_group(i - lag_e - LAST0 - 1)
        return carry

    lax.fori_loop(0, STEP_COUNT + NY + 4 + 1, body, 0)
    mode[0] = "start"
    for xx in range(NX):
        piece(1, xx)
    scatter(1)

    got(lbuf.at[:, :, :, pl.ds(3 * (1 - k), 3)], sib_r.at[NG + 5])

    def factor(q):
        return jnp.concatenate([lbuf[p, :, :, 2 * q : 2 * q + 2].reshape(B, 128) for p in range(4)], 1)

    def tile(q):
        return lambda i, j: lbuf[j, 2 * i : 2 * i + 2, :, 2 * q : 2 * q + 2].reshape(128, 128)

    invert(tile(0), v1)
    invert(tile(1), v2)
    v1t[...] = v1[...].T
    v2t[...] = v2[...].T
    mmat[...] = mm(factor(2), v1[...])
    mt[...] = mmat[...].T
    for q in range(3):
        ltr[q] = lloc[q].T
    for s in range(1, NZ):
        frm = up(z, s, NZ)
        got(cgb.at[frm], cr.at[frm])
    mine = pl.ds(pl.multiple_of(z * 64, 64), 64)

    def cross_half(lo):
        return jnp.concatenate([cgb[c // 2, c % 2, :, 0:64] for c in range(lo, lo + NZ)], 1)

    @pl.when(first)
    def _():
        corner = jnp.concatenate([cgb[c // 2, c % 2, :, 64:96] for c in range(2 * NZ)], 1)
        cross = split(cross_half(0))
        fold[0] = mm(ltr[0, mine, :], corner) + mm_split(split(ltr[2, mine, :]), cross)
        fold[1] = mm_split(split(ltr[1, mine, :]), cross)

    @pl.when(k == 1)
    def _():
        fold[0] = mm(ltr[1, mine, :], cross_half(NZ))

    fcopy.wait()
    got(fbuf.at[1 - k], sib_r.at[NG + 1])
    for g in range(NG):
        for s in range(1, NZ):
            frm = up(z, s, NZ)
            got(sbuf.at[g, frm], sr.at[g, frm])
        total = sbuf[g, 0]
        for s in range(1, NZ):
            total = total + sbuf[g, s]
        lanes = slice(g * W, g * W + W)
        xr[:, :, lanes] = fbuf[:, :, lanes] - 2.0 * total.reshape(2, ROWS, W)

    xall = xr[...].reshape(2 * ROWS, B)
    for s in range(NZ):
        xst[s] = xall[:, 64 * s : 64 * s + 64]
    for s in range(1, NZ):
        to = up(z, s, NZ)
        put(xst.at[to], xs.at[z], as_.at[s], ar.at[z], zpeer[s - 1])
    put(xr.at[1 - k], xo.at[k], sib_s.at[NG + 2], sib_r.at[NG + 2], sib)
    xo[k] = xr[k]
    xs[z] = xst[z]
    for s in range(1, NZ):
        frm = up(z, s, NZ)
        got(xs.at[frm], ar.at[frm])
    put(xs, xs2, sib_s.at[NG + 3], sib_r.at[NG + 3], sib, k == 1)

    def gram(b, src):
        a = split(src[...].reshape(NZ * 64, 64).T)
        for g in range(NG):
            bb = split(band[g].reshape(NZ * 64, W))
            lanes = slice(g * W, g * W + W)
            gm[b, :, :, lanes] = (mm_split(a, bb) - fold[b, :, lanes]).reshape(NY, 8, W)

    def plane_reduce_start(b, cond):
        for s in range(1, NY):
            to = up(y, s, NY)
            put(gm.at[b, to], gy.at[b, y], gys.at[b, s], gyr.at[b, y], ypeer[s - 1], cond)

    gram(0, xs)
    plane_reduce_start(0, None)

    @pl.when(first)
    def _():
        got(xs2, sib_r.at[NG + 3])
        gram(1, xs2)

    plane_reduce_start(1, first)
    conds = (None, first)

    def when(cond, fn):
        if cond is None:
            fn()
        else:
            pl.when(cond)(fn)

    def y_sum(b):
        gy[b, y] = gm[b, y]
        for s in range(1, NY):
            frm = up(y, s, NY)
            got(gy.at[b, frm], gyr.at[b, frm])
        total = gy[b, 0]
        for s in range(1, NY):
            total = total + gy[b, s]
        sg[b] = total
        gx[b, x] = total

    def x_sum(b):
        for s in range(1, NX):
            frm = up(x, s, NX)
            got(gx.at[b, frm], gxr.at[b, frm])
        total = (gx[b, 0] + gx[b, 1]) + (gx[b, 2] + gx[b, 3])
        gz[b, 0, z, y] = total[:, 0:W2]
        gz[b, 1, z, y] = total[:, W2:B]

    def y_wait(b):
        for s in range(1, NY):
            frm = up(y, s, NY)
            got(gz.at[b, 0, z, frm], gar.at[b, frm])
        for s in range(1, NZ):
            frm = up(z, s, NZ)
            got(gz.at[b, 1, frm, y], gbr.at[b, frm])

    for b in range(2):
        when(conds[b], functools.partial(y_sum, b))
        for s in range(1, NX):
            put(sg.at[b], gx.at[b, x], gxs.at[b, s], gxr.at[b, x], xpeer[s - 1], conds[b])
    got(xo.at[1 - k], sib_r.at[NG + 2])
    h2 = mm(xo[1], v2[...])
    rows_ref[:, B : 2 * B] = h2
    rows_ref[:, 0:B] = mm(xo[0], v1[...]) - mm(h2, mmat[...])

    for b in range(2):
        when(conds[b], functools.partial(x_sum, b))
        for s in range(1, NY):
            put(gz.at[b, 0, z, y], gz.at[b, 0, z, y], gas.at[b, s], gar.at[b, y], ypeer[s - 1], conds[b])
        for s in range(1, NZ):
            put(gz.at[b, 1, z, y], gz.at[b, 1, z, y], gbs.at[b, s], gbr.at[b, z], zpeer[s - 1], conds[b])
    for j in range(NZ):
        zz, yy = up(z, ORDER[j], NZ), up(y, ORDER[j], NY)
        hop = abs(ORDER[j])
        for b in range(2):
            chunk, other = gz.at[b, 0, zz], gz.at[b, 1, :, yy]
            if j == 0:
                when(conds[b], functools.partial(y_wait, b))
            else:
                when(conds[b], functools.partial(got, chunk, gzr.at[b, zz]))
                when(conds[b], functools.partial(got, other, gwr.at[b, yy]))
            if j == 0 or (ORDER[j] < 0 and hop < NZ // 2):
                put(chunk, chunk, gzs.at[0, b, hop], gzr.at[b, zz], zup, conds[b])
                put(other, other, gws.at[0, b, hop], gwr.at[b, yy], yup, conds[b])
            if j == 0 or (ORDER[j] > 0 and hop < NZ // 2 - 1):
                put(chunk, chunk, gzs.at[1, b, hop], gzr.at[b, zz], zdn, conds[b])
                put(other, other, gws.at[1, b, hop], gwr.at[b, yy], ydn, conds[b])

    def gram_total(b):
        return jnp.concatenate([gz[b, 0].reshape(B, W2), gz[b, 1].reshape(B, W2)], 1)

    r = lax.broadcasted_iota(jnp.int32, (B, B), 0)
    c = lax.broadcasted_iota(jnp.int32, (B, B), 1)
    own = pl.ds(pl.multiple_of(row * 16, 16), 16)

    def lowered(p):
        return jnp.where(r > c, p, jnp.where(r == c, 0.5 * p, 0.0))

    @pl.when(k == 1)
    def _():
        left = split(v2t[...])
        p2 = mm_split(left, split(gram_total(0)))
        q2 = lowered(mm(factor(1).T, jnp.where(r >= c, -p2, 0.0)))
        w1[...] = mm(q2 + q2.T, v2[...])
        sbm[...] = 0.5 * mm_split(left, split(w1[...]))

    put(sbm, sbm, sib_s.at[NG + 6], sib_r.at[NG + 6], sib, k == 1)

    @pl.when(first)
    def _():
        p1 = split(-mm(v2t[...], gram_total(1)))
        w1[...] = mm_split(p1, split(v1[...]))
        w2[...] = mm(v1t[...], gram_total(0)) + mm_split(split(mt[...]), p1)
        got(sbm, sib_r.at[NG + 6])
        coupling = w1[...] - 2.0 * mm(sbm[...], mmat[...])
        cpl[...] = coupling
        outp[0] = cpl[own, :]
        grad = jnp.where(r >= c, -w2[...] - mm(coupling.T, factor(2)), 0.0)
        q1 = lowered(mm(factor(0).T, grad))
        w1[...] = q1 + q1.T
        outp[1] = 0.5 * mm(mm(v1t[own, :], w1[...]), v1[...])

    put(outp, outp, sib_s.at[NG + 7], sib_r.at[NG + 7], sib, first)

    @pl.when(k == 1)
    def _():
        got(outp, sib_r.at[NG + 7])

    shift = lax.rem(B - col * 32, B)
    c_ref[...] = pltpu.roll(outp[0], shift, 1)[:, 0:32]
    b_ref[0] = pltpu.roll(outp[1], shift, 1)[:, 0:32]
    b_ref[1] = pltpu.roll(sbm[own, :], shift, 1)[:, 0:32]

    for c, cond in sends:
        if cond is None:
            c.wait_send()
        else:
            pl.when(cond)(c.wait_send)
    mode[0] = "finish"
    for task in background.values():
        task()
    scatter(0)

    def sent(n, carry):
        stage_a(n)
        stage_b(n)
        stage_d(n)
        return carry

    lax.fori_loop(0, STEP_COUNT, sent, 0)


def panel_call(*args):
    dma = pltpu.SemaphoreType.DMA
    vm = pl.BlockSpec(memory_space=pltpu.VMEM)
    hbm = pl.BlockSpec(memory_space=pl.ANY)
    square = pltpu.VMEM((B, B), F32)
    return pl.pallas_call(
        panel_kernel,
        out_shape=(
            jax.ShapeDtypeStruct((ROWS, 2 * B), F32),
            jax.ShapeDtypeStruct((2, 16, 32), F32),
            jax.ShapeDtypeStruct((16, 32), F32),
        ),
        in_specs=[hbm] * 7,
        out_specs=(vm, vm, vm),
        scratch_shapes=[
            pltpu.VMEM((2, 512, 1024), F32),
            pltpu.VMEM((NX, 512, 512), BF16),
            pltpu.VMEM((NX, 512, 512), BF16),
            pltpu.VMEM((NG, NZ, 2, ROWS, W), F32),
            pltpu.VMEM((NG, NX, NZ, 2, ROWS, W), F32),
            pltpu.VMEM((NG, NZ, 2 * ROWS, W), F32),
            pltpu.VMEM((NG, NZ, 2 * ROWS, W), F32),
            pltpu.VMEM((2, ROWS, B), F32),
            pltpu.VMEM((2, ROWS, B), F32),
            pltpu.VMEM((2, ROWS, B), F32),
            pltpu.VMEM((NZ, 64, 64), F32),
            pltpu.VMEM((NZ, 64, 64), F32),
            pltpu.VMEM((NZ, 64, 64), F32),
            pltpu.VMEM((2, NY, 8, B), F32),
            pltpu.VMEM((2, NY, 8, B), F32),
            pltpu.VMEM((2, 8, B), F32),
            pltpu.VMEM((2, NX, 8, B), F32),
            pltpu.VMEM((2, 2, NZ, NY, 8, W2), F32),
            pltpu.VMEM((3, 16, B), F32),
            pltpu.VMEM((16, 64), F32),
            pltpu.VMEM((16, 32), F32),
            pltpu.VMEM((4, NY, NX, 6, 8, 128), F32),
            pltpu.VMEM((NZ, 2, 16, 128), F32),
            pltpu.VMEM((3, B, 16), F32),
            pltpu.VMEM((2, 64, B), F32),
        ]
        + [square] * 10
        + [
            pltpu.VMEM((2, 16, B), F32),
            dma((NG + 8,)), dma((NG + 8,)), dma((NG + 6,)),
            dma((2, NG, NZ)), dma((NG, NZ)),
            dma((2, NG, NZ)), dma((3, NG, NZ)), dma((NG, NX, NZ)),
            dma((NG, NZ)), dma((NG, NZ)),
            dma((NZ,)), dma((NZ,)),
            dma((2, NY)), dma((2, NY)),
            dma((2, NX)), dma((2, NX)),
            dma((2, NY)), dma((2, NY)),
            dma((2, NZ)), dma((2, NZ)),
            dma((2, 2, NZ // 2)), dma((2, NZ)),
            dma((2, 2, NY // 2)), dma((2, NY)),
            dma((NX,)), dma((NX,)), dma((NY,)), dma((NY,)),
            dma((2,)), dma((2,)), dma((2,)), dma((2,)),
            dma((NZ,)), dma((NZ,)),
        ],
        compiler_params=pltpu.CompilerParams(
            collective_id=0, has_side_effects=True, vmem_limit_bytes=52 * 1024 * 1024
        ),
        name="panel_adjoint",
    )(*args)


def invert(lower, out_ref):
    n = 128
    r = lax.broadcasted_iota(jnp.int32, (n, n), 0)
    c = lax.broadcasted_iota(jnp.int32, (n, n), 1)
    blocks = [lower(q, q) for q in range(4)]
    inv = []
    for a in blocks:
        diag = jnp.sum(jnp.where(r == c, a, 0.0), axis=1, keepdims=True)
        inv.append(jnp.where(r == c, 1.0 / diag, 0.0))
    for lb in range(7):
        mask = ((r >> (lb + 1)) == (c >> (lb + 1))) & ((r >> lb) > (c >> lb))
        for q in range(4):
            cut = jnp.where(mask, blocks[q], 0.0)
            yy = split(inv[q])
            inv[q] = inv[q] - mm_split(yy, split(mm_split(split(cut), yy)))
    zero = jnp.zeros((n, n), F32)
    wide = []
    for h in range(2):
        a, b = inv[2 * h], inv[2 * h + 1]
        low = -mm(b, mm(lower(2 * h + 1, 2 * h), a))
        wide.append(jnp.concatenate([jnp.concatenate([a, zero], 1), jnp.concatenate([low, b], 1)], 0))
    corner = jnp.concatenate(
        [jnp.concatenate([lower(2, 0), lower(2, 1)], 1), jnp.concatenate([lower(3, 0), lower(3, 1)], 1)], 0
    )
    low = -mm(wide[1], mm(corner, wide[0]))
    out_ref[0:256, 0:256] = wide[0]
    out_ref[0:256, 256:512] = jnp.zeros((256, 256), F32)
    out_ref[256:512, 0:256] = low
    out_ref[256:512, 256:512] = wide[1]


def per_device(*args):
    return panel_call(*args)


def solution(mesh):
    return jax.shard_map(
        per_device,
        mesh=mesh,
        in_specs=(
            P("row", "col"),
            P(("row", "col"), None),
            P(("row", "col"), None),
            P(None, "row", None),
            P("row", None),
            P("row", "col"),
            P("row", "col"),
        ),
        out_specs=(P(("row", "col"), None), P(None, "row", "col"), P("row", "col")),
        check_vma=False,
    )
```

time: 241 us -> 163 us (0.68)
  blocking collectives: 40.1 us -> 0 us
  Pallas kernels: 178 us -> 155 us
  between operations: 14.1 us -> 0.66 us
    all_gather x2 -> x0, blocking collectives: 40.1 us -> none  [the longest x1 25.1 us: per_device(): cross_wide = lax.all_gather(cross_grad, 'col', axis=1, tiled=True)]
    pallas_call x2 -> x1, Pallas kernels: 178 us -> 155 us  [panel_call(): pl.pallas_call(panel_kernel, out_shape=(jax.ShapeDtypeStruct((ROWS, 2 * B...]
    unnamed x10 -> x15, local copies, waits for them, and re-layouts: 4.76 us -> 6.65 us
  transfers between devices with their start and end apart: 1 -> 0, of which waited for: 0 -> 0; matrix products, arithmetic and copies ran while one was open for 1% -> 0% of each run, Pallas kernels for 65% -> 0%
where the time goes in v2:
time: 163 us
  Pallas kernels  155 us (95%)
  local copies, waits for them, and re-layouts  6.65 us (4%)
    pallas_call x1, Pallas kernels, panel_call(): pl.pallas_call(panel_kernel, out_shape=(jax.ShapeDtypeStruct((ROWS, 2 * B...  155 us
    unnamed x15, local copies, waits for them, and re-layouts  6.65 us

profile of v2, /device:TPU:1, one launch (start us, length us, event | category | flops | bytes accessed | tf_op | source)
XLA Modules:
  0.0 162.7 jit_solution(2406856164189866170)
XLA Ops:
  0.6 0.0 copy-start
  0.6 0.9 copy-done
  1.5 0.0 copy-start.1
  1.5 0.9 copy-done.1
  2.4 0.0 copy-start.2
  2.4 0.8 copy-done.2
  3.3 0.0 copy-start.3
  3.3 0.8 copy-done.3
  4.0 0.0 copy-start.4
  4.0 0.7 copy-done.4
  4.7 0.0 copy-start.5
  4.7 0.7 copy-done.5
  5.4 155.4 %panel_adjoint.1 = (f32[32,1024]{1,0:T(8,128)S(1)}, f32[2,16,32]{2,1,0:T(8,128)S(1)}, f32[16,32]{1,0:T(8,128)S(1)}) custom-call(f32[512,1024]{1,0:T(8,128)} %t_ref.1, f32[32,1024]{1,0:T(8,128)S(1)} %copy-done, f32[32,1024]{1,0:T(8,128)S(1)} %copy-done.1, f32[2,16,512]{2,1,0:T(8,128)S(1)} %copy-done.2, f32[16,512]{1,0:T(8,128)S(1)} %copy-done.3, ...), custom_call_target="tpu_custom_call" | custom-call | tf_op jit(solution)/shard_map/panel_adjoint/pallas_call | solution.py:512
  160.8 0.7 copy.13
  161.5 0.6 copy.14
  162.1 0.6 copy.15
Async XLA Ops:
  0.6 0.9 copy-start
  1.5 0.9 copy-start.1
  2.4 0.8 copy-start.2
  3.3 0.8 copy-start.3
  4.0 0.7 copy-start.4
  4.7 0.7 copy-start.5

commit v3 on v2

--- a/solution.py
+++ b/solution.py
@@ -17,9 +17,9 @@
 W2 = B // 2
 ROWS = 32
 ORDER = (0, -1, 1, -2, 2, -3, 3, -4)
-STEPS = sorted(((g, o) for g in range(NG) for o in ORDER), key=lambda s: (abs(s[1]) + 2 * s[0], s[0]))
+STEPS = [(g, o) for g in range(NG) for o in ORDER]
 STEP_COUNT = len(STEPS)
-LAST0 = max(i for i, s in enumerate(STEPS) if s[0] == 0)
+LAST0 = NZ - 1
 
 
 def pick(values, n):
@@ -50,7 +50,7 @@
     tbuf, thi, tlo, band, rbuf, psum, sbuf, fbuf, xr, xo, xst, xs, xs2, gm, gy, sg, gx, gz,
     lloc, cgl, col_, lbuf, cgb, ltr, fold, v1, v2, v1t, v2t, mmat, mt, w1, w2, sbm, cpl, outp,
     sib_s, sib_r, loc, zs, zr, ys, xsm, rr, ss, sr, as_, ar, gys, gyr, gxs, gxr, gas, gar, gbs, gbr, gzs, gzr,
-    gws, gwr, lxs, lxr, lys, lyr, lzs, lzr, lfs, lfr, cs_, cr,
+    gws, gwr, lys, lyr, lzs, lzr, lfs, lfr, cs_, cr,
 ):
     local = [
         pltpu.make_async_copy(diag_ref, lloc.at[pl.ds(0, 2)], loc.at[1]),
@@ -84,7 +84,15 @@
     partners = [sib] + zpeer + ypeer + xpeer
     for p in partners:
         pl.semaphore_signal(barrier, inc=1, device_id=p, device_id_type=MESH)
-    pl.semaphore_wait(barrier, len(partners))
+
+    swap = [dev(x, z, y, k), dev(x, z, y, 1 - k)]
+
+    @pl.when(d != 0)
+    def _():
+        for p in swap:
+            pl.semaphore_signal(barrier, inc=1, device_id=p, device_id_type=MESH)
+
+    pl.semaphore_wait(barrier, len(partners) + jnp.where(d == 0, 0, 2))
 
     sends = []
     mode = ["start"]
@@ -108,14 +116,20 @@
             ).wait_recv()
 
     first = k == 0
-    for g in range(NG):
-        lanes = pl.ds(pl.multiple_of((1 - k) * B + g * W, 128), W)
-        put(r_ref.at[:, lanes], band.at[g, z, k], sib_s.at[g], sib_r.at[g], sib)
     rcopies = []
     for g in range(NG):
-        lanes = pl.ds(pl.multiple_of(k * B + g * W, 128), W)
-        rcopies.append(pltpu.make_async_copy(r_ref.at[:, lanes], band.at[g, z, k], loc.at[5 + g]))
-        rcopies[-1].start()
+        ours = r_ref.at[:, pl.ds(pl.multiple_of(k * B + g * W, 128), W)]
+        theirs = r_ref.at[:, pl.ds(pl.multiple_of((1 - k) * B + g * W, 128), W)]
+        slot, sem = rbuf.at[g, x, z, k], rr.at[g, x, z]
+        put(ours, slot, sib_s.at[NG + 8 + g], sem, swap[0], d != 0)
+        put(theirs, slot, sib_s.at[NG + 10 + g], sem, swap[1])
+        rcopies.append((pltpu.make_async_copy(ours, slot, sem), d == 0))
+        pl.when(d == 0)(rcopies[-1][0].start)
+    for g in range(NG):
+        ours = r_ref.at[:, pl.ds(pl.multiple_of(k * B + g * W, 128), W)]
+        theirs = r_ref.at[:, pl.ds(pl.multiple_of((1 - k) * B + g * W, 128), W)]
+        put(theirs, band.at[g, z, k], sib_s.at[g], sib_r.at[g], sib)
+        pltpu.make_async_copy(ours, band.at[g, z, k], loc.at[5 + g]).start()
     put(t_ref, tbuf.at[k], sib_s.at[NG], sib_r.at[NG], sib)
     tcopy = pltpu.make_async_copy(t_ref, tbuf.at[k], loc.at[0])
     tcopy.start()
@@ -124,51 +138,38 @@
     fcopy.start()
     for c in local:
         c.wait()
-    quarter = lax.rem(z, 4)
     half = pl.ds(3 * k, 3)
-    for p in range(4):
-
-        @pl.when(quarter == p)
-        def _():
-            for q in range(3):
-                lbuf[p, y, x, 2 * q : 2 * q + 2] = lloc[q, :, 128 * p : 128 * p + 128].reshape(2, 8, 128)
-
-    for s in range(1, NX):
-        put(
-            lbuf.at[quarter, y, x, half], lbuf.at[quarter, y, x, half], lxs.at[s], lxr.at[x], xpeer[s - 1]
-        )
+    for q in range(3):
+        for p in range(4):
+            lbuf[p, y, x, 2 * q : 2 * q + 2] = lloc[q, :, 128 * p : 128 * p + 128].reshape(2, 8, 128)
     cgb[z, k] = jnp.zeros((16, 128), F32)
     cgb[z, k, :, 0:64] = cgl[...]
     cgb[z, k, :, 64:96] = col_[...]
     put(cgb.at[z, k], cgb.at[z, k], sib_s.at[NG + 4], sib_r.at[NG + 4], sib)
 
     def l_rows():
-        for s in range(1, NX):
-            frm = up(x, s, NX)
-            got(lbuf.at[quarter, y, frm, half], lxr.at[frm])
+        part = lbuf.at[:, y, x, half]
         for s in range(1, NY):
-            put(lbuf.at[quarter, y, :, half], lbuf.at[quarter, y, :, half], lys.at[s], lyr.at[y], ypeer[s - 1])
+            put(part, part, lys.at[s], lyr.at[y], ypeer[s - 1])
 
     def l_planes():
         for s in range(1, NY):
             frm = up(y, s, NY)
-            got(lbuf.at[quarter, frm, :, half], lyr.at[frm])
-        for i, to in enumerate((zup, zdn)):
-            put(lbuf.at[quarter, :, :, half], lbuf.at[quarter, :, :, half], lzs.at[i], lzr.at[i], to)
+            got(lbuf.at[:, frm, x, half], lyr.at[frm])
+        part = lbuf.at[:, :, x, half]
+        for i, to in enumerate((xup, xdn)):
+            put(part, part, lzs.at[i], lzr.at[i], to)
 
     def l_far():
-        below, above = up(quarter, 3, 4), up(quarter, 1, 4)
-        got(lbuf.at[below, :, :, half], lzr.at[0])
-        part = lbuf.at[below, pl.ds(0, NY // 2), :, half]
-        put(part, part, lfs.at[0], lfr.at[0], zup)
-        got(lbuf.at[above, :, :, half], lzr.at[1])
-        part = lbuf.at[above, pl.ds(NY // 2, NY // 2), :, half]
-        put(part, part, lfs.at[1], lfr.at[1], zdn)
+        for i, (to, frm) in enumerate(((xup, up(x, -1, NX)), (xdn, up(x, 1, NX)))):
+            got(lbuf.at[:, :, frm, half], lzr.at[i])
+            part = lbuf.at[pl.ds(2 * i, 2), :, frm, half]
+            put(part, part, lfs.at[i], lfr.at[i], to)
 
     def l_cores():
-        far = up(quarter, 2, 4)
+        far = up(x, 2, NX)
         for i in range(2):
-            got(lbuf.at[far, pl.ds(i * NY // 2, NY // 2), :, half], lfr.at[i])
+            got(lbuf.at[pl.ds(2 * i, 2), :, far, half], lfr.at[i])
         put(lbuf.at[:, :, :, half], lbuf.at[:, :, :, half], sib_s.at[NG + 5], sib_r.at[NG + 5], sib)
 
     def adjoint_rows():
@@ -176,51 +177,40 @@
         for s in range(1, NZ):
             put(cgb.at[z], cgb.at[z], cs_.at[s], cr.at[z], zpeer[s - 1])
 
-    hops = jnp.where(d <= NY // 2, d, NY - d)
-    lag_b = 2 * hops
-    lag_d = lag_b + 2
-    lag_e = lag_d + 2
-    background = {2: l_rows, 8: l_planes, 10: adjoint_rows, 16: l_far, 20: l_cores}
+    lag_d = 2
+    lag_e = 4
+
+    def band_ring(hop):
+        low, high = up(z, -hop, NZ), up(z, hop, NZ)
+        if hop == 0:
+            if mode[0] != "finish":
+                for g in range(NG):
+                    ours = band.at[g, z, k]
+                    pltpu.make_async_copy(ours, ours, loc.at[5 + g]).wait()
+                    got(band.at[g, z, 1 - k], sib_r.at[g])
+        else:
+            got(band.at[:, low], zr.at[low])
+            if hop < NZ // 2:
+                got(band.at[:, high], zr.at[high])
+        if hop < NZ // 2:
+            put(band.at[:, low], band.at[:, low], zs.at[0, hop], zr.at[low], zup)
+        if hop < NZ // 2 - 1:
+            put(band.at[:, high], band.at[:, high], zs.at[1, hop], zr.at[high], zdn)
+
+    background = [(3, adjoint_rows), (13, l_rows)]
+    background += [(5 + 3 * h, functools.partial(band_ring, h)) for h in range(NZ // 2 + 1)]
 
     def step(n):
         o = pick([st[1] + 4 for st in STEPS], n)
-        return pick([st[0] for st in STEPS], n), o, lax.rem(z + o + NZ - 4, NZ)
-
-    def stage_a(n):
-        g, o, zz = step(n)
-        if mode[0] != "finish":
-
-            @pl.when(o == 4)
-            def _():
-                pltpu.make_async_copy(band.at[g, z, k], band.at[g, z, k], loc.at[5 + g]).wait()
-                got(band.at[g, z, 1 - k], sib_r.at[g])
-
-            @pl.when(o != 4)
-            def _():
-                got(band.at[g, zz], zr.at[g, zz])
-
-        chunk = band.at[g, zz]
-        put(chunk, chunk, zs.at[0, g, o], zr.at[g, zz], zup, jnp.logical_and(o >= 1, o <= 4))
-        put(chunk, chunk, zs.at[1, g, o], zr.at[g, zz], zdn, jnp.logical_and(o >= 4, o <= 6))
-        put(chunk, rbuf.at[g, x, zz], ys.at[0, g, o], rr.at[g, x, zz], yup, d == 0)
-        put(chunk, rbuf.at[g, x, zz], ys.at[1, g, o], rr.at[g, x, zz], ydn, d == 0)
-        if mode[0] != "finish":
-
-            @pl.when(d == 0)
-            def _():
-                rbuf[g, x, zz] = band[g, zz]
+        return pick([st[0] for st in STEPS], n), o, lax.rem(y + o + NZ - 4, NZ)
 
     def stage_b(n):
         g, o, zz = step(n)
         slot, sem = rbuf.at[g, x, zz], rr.at[g, x, zz]
-        if mode[0] != "finish":
-
-            @pl.when(d != 0)
-            def _():
-                got(slot, sem)
-
-        put(slot, slot, ys.at[0, g, o], sem, yup, jnp.logical_and(d >= 1, d <= 3))
-        put(slot, slot, ys.at[1, g, o], sem, ydn, d >= 6)
+        got(slot, sem)
+
+        put(slot, slot, ys.at[0, g, o], sem, yup, jnp.logical_and(o >= 1, o <= 4))
+        put(slot, slot, ys.at[1, g, o], sem, ydn, jnp.logical_and(o >= 4, o <= 6))
         put(slot, slot, xsm.at[0, g, o], sem, xup)
         put(slot, slot, xsm.at[1, g, o], sem, xdn)
 
@@ -257,54 +247,42 @@
             fn(n)
 
     def first_group(n):
-        @pl.when(n == 0)
-        def _():
-            tcopy.wait()
-            got(tbuf.at[1 - k], sib_r.at[NG])
-
         @pl.when(jnp.logical_and(n >= 0, n < NX))
         def _():
-            lanes = pl.ds(pl.multiple_of(lax.rem(n, 2) * 512, 128), 512)
-            thi[n], tlo[n] = split(tbuf[n // 2, :, lanes])
             piece(0, n)
 
         @pl.when(n == NX)
         def _():
             scatter(0)
 
+    def split_t(h):
+        for i in range(2):
+            thi[2 * h + i], tlo[2 * h + i] = split(tbuf[h, :, 512 * i : 512 * i + 512])
+
+    tcopy.wait()
+    got(tbuf.at[1 - k], sib_r.at[NG])
+    for h in range(2):
+        split_t(h)
     psum[...] = jnp.zeros_like(psum)
     mode[0] = "loop"
 
     def body(i, carry):
-        for at, task in background.items():
-            pl.when(i == at)(task)
-        within(i, stage_a)
-        within(i - lag_b, stage_b)
+        within(i, stage_b)
         within(i - lag_d, stage_d)
         within(i - lag_e, stage_e)
+        for at, task in background:
+            pl.when(i == at)(task)
         first_group(i - lag_e - LAST0 - 1)
         return carry
 
-    lax.fori_loop(0, STEP_COUNT + NY + 4 + 1, body, 0)
+    lax.fori_loop(0, STEP_COUNT + 4, body, 0)
     mode[0] = "start"
+    l_planes()
     for xx in range(NX):
         piece(1, xx)
     scatter(1)
-
-    got(lbuf.at[:, :, :, pl.ds(3 * (1 - k), 3)], sib_r.at[NG + 5])
-
-    def factor(q):
-        return jnp.concatenate([lbuf[p, :, :, 2 * q : 2 * q + 2].reshape(B, 128) for p in range(4)], 1)
-
-    def tile(q):
-        return lambda i, j: lbuf[j, 2 * i : 2 * i + 2, :, 2 * q : 2 * q + 2].reshape(128, 128)
-
-    invert(tile(0), v1)
-    invert(tile(1), v2)
-    v1t[...] = v1[...].T
-    v2t[...] = v2[...].T
-    mmat[...] = mm(factor(2), v1[...])
-    mt[...] = mmat[...].T
+    l_far()
+
     for q in range(3):
         ltr[q] = lloc[q].T
     for s in range(1, NZ):
@@ -344,6 +322,7 @@
     for s in range(1, NZ):
         to = up(z, s, NZ)
         put(xst.at[to], xs.at[z], as_.at[s], ar.at[z], zpeer[s - 1])
+    l_cores()
     put(xr.at[1 - k], xo.at[k], sib_s.at[NG + 2], sib_r.at[NG + 2], sib)
     xo[k] = xr[k]
     xs[z] = xst[z]
@@ -412,10 +391,32 @@
         when(conds[b], functools.partial(y_sum, b))
         for s in range(1, NX):
             put(sg.at[b], gx.at[b, x], gxs.at[b, s], gxr.at[b, x], xpeer[s - 1], conds[b])
-    got(xo.at[1 - k], sib_r.at[NG + 2])
-    h2 = mm(xo[1], v2[...])
-    rows_ref[:, B : 2 * B] = h2
-    rows_ref[:, 0:B] = mm(xo[0], v1[...]) - mm(h2, mmat[...])
+    def factor(q):
+        return jnp.concatenate([lbuf[p, :, :, 2 * q : 2 * q + 2].reshape(B, 128) for p in range(4)], 1)
+
+    def tile(q):
+        return lambda i, j: lbuf[j, 2 * i : 2 * i + 2, :, 2 * q : 2 * q + 2].reshape(128, 128)
+
+    def second_inverse():
+        got(lbuf.at[:, :, :, pl.ds(3 * (1 - k), 3)], sib_r.at[NG + 5])
+        invert(tile(1), v2)
+
+    def first_inverse():
+        v2t[...] = v2[...].T
+        invert(tile(0), v1)
+
+    def coupling_factor():
+        v1t[...] = v1[...].T
+        mmat[...] = mm(factor(2), v1[...])
+
+    def tall_rows():
+        mt[...] = mmat[...].T
+        got(xo.at[1 - k], sib_r.at[NG + 2])
+        h2 = mm(xo[1], v2[...])
+        rows_ref[:, B : 2 * B] = h2
+        rows_ref[:, 0:B] = mm(xo[0], v1[...]) - mm(h2, mmat[...])
+
+    between = {0: first_inverse, 2: coupling_factor, 4: tall_rows}
 
     for b in range(2):
         when(conds[b], functools.partial(x_sum, b))
@@ -423,6 +424,7 @@
             put(gz.at[b, 0, z, y], gz.at[b, 0, z, y], gas.at[b, s], gar.at[b, y], ypeer[s - 1], conds[b])
         for s in range(1, NZ):
             put(gz.at[b, 1, z, y], gz.at[b, 1, z, y], gbs.at[b, s], gbr.at[b, z], zpeer[s - 1], conds[b])
+    second_inverse()
     for j in range(NZ):
         zz, yy = up(z, ORDER[j], NZ), up(y, ORDER[j], NY)
         hop = abs(ORDER[j])
@@ -439,6 +441,8 @@
             if j == 0 or (ORDER[j] > 0 and hop < NZ // 2 - 1):
                 put(chunk, chunk, gzs.at[1, b, hop], gzr.at[b, zz], zdn, conds[b])
                 put(other, other, gws.at[1, b, hop], gwr.at[b, yy], ydn, conds[b])
+        if j in between:
+            between[j]()
 
     def gram_total(b):
         return jnp.concatenate([gz[b, 0].reshape(B, W2), gz[b, 1].reshape(B, W2)], 1)
@@ -491,12 +495,11 @@
         else:
             pl.when(cond)(c.wait_send)
     mode[0] = "finish"
-    for task in background.values():
+    for _, task in background:
         task()
     scatter(0)
 
     def sent(n, carry):
-        stage_a(n)
         stage_b(n)
         stage_d(n)
         return carry
@@ -548,8 +551,8 @@
         + [square] * 10
         + [
             pltpu.VMEM((2, 16, B), F32),
-            dma((NG + 8,)), dma((NG + 8,)), dma((NG + 6,)),
-            dma((2, NG, NZ)), dma((NG, NZ)),
+            dma((NG + 12,)), dma((NG + 8,)), dma((NG + 6,)),
+            dma((2, NZ)), dma((NZ,)),
             dma((2, NG, NZ)), dma((3, NG, NZ)), dma((NG, NX, NZ)),
             dma((NG, NZ)), dma((NG, NZ)),
             dma((NZ,)), dma((NZ,)),
@@ -559,12 +562,12 @@
             dma((2, NZ)), dma((2, NZ)),
             dma((2, 2, NZ // 2)), dma((2, NZ)),
             dma((2, 2, NY // 2)), dma((2, NY)),
-            dma((NX,)), dma((NX,)), dma((NY,)), dma((NY,)),
+            dma((NY,)), dma((NY,)),
             dma((2,)), dma((2,)), dma((2,)), dma((2,)),
             dma((NZ,)), dma((NZ,)),
         ],
         compiler_params=pltpu.CompilerParams(
-            collective_id=0, has_side_effects=True, vmem_limit_bytes=52 * 1024 * 1024
+            collective_id=0, has_side_effects=True, vmem_limit_bytes=60 * 1024 * 1024
         ),
         name="panel_adjoint",
     )(*args)

time: 163 us -> 148 us (0.908)
  Pallas kernels: 155 us -> 143 us
  local copies, waits for them, and re-layouts: 6.65 us -> 4.19 us
    pallas_call x1, Pallas kernels: 155 us -> 143 us  [panel_call(): pl.pallas_call(panel_kernel, out_shape=(jax.ShapeDtypeStruct((ROWS, 2 * B...]
    unnamed x15 -> x3, local copies, waits for them, and re-layouts: 6.65 us -> 4.19 us
where the time goes in v3:
time: 148 us; the launch traced here: 147 us
  Pallas kernels  143 us (97%)
  local copies, waits for them, and re-layouts  4.19 us (3%)
    pallas_call x1, Pallas kernels, panel_call(): pl.pallas_call(panel_kernel, out_shape=(jax.ShapeDtypeStruct((ROWS, 2 * B...  143 us
    unnamed x3, local copies, waits for them, and re-layouts  4.19 us

profile of v3, /device:TPU:1, one launch (start us, length us, event | category | flops | bytes accessed | tf_op | source)
XLA Modules:
  0.0 147.4 jit_solution(6716391990726264683)
XLA Ops:
  0.6 142.5 %panel_adjoint.1 = (f32[32,1024]{1,0:T(8,128)}, f32[2,16,32]{2,1,0:T(8,128)}, f32[16,32]{1,0:T(8,128)}) custom-call(f32[512,1024]{1,0:T(8,128)} %t_ref.1, f32[32,1024]{1,0:T(8,128)} %r_ref.1, f32[32,1024]{1,0:T(8,128)} %f_ref.1, f32[2,16,512]{2,1,0:T(8,128)} %diag_ref.1, f32[16,512]{1,0:T(8,128)} %cross_ref.1, f32[16,64]{1,0:T(8,128)} %cg_ref.1, f32[16,32]{1,0:T(8,128)} %co_ref.1), custom_call_target="tpu_custom_call" | custom-call | tf_op jit(solution)/shard_map/panel_adjoint/pallas_call | solution.py:515
  143.2 1.6 %copy.13 = f32[32,1024]{1,0:T(8,128)} copy(f32[32,1024]{1,0:T(8,128)} %get-tuple-element.6) | data formatting | bytes 262144
  144.8 1.3 copy.14
  146.1 1.3 copy.15

commit v4 on v3

--- a/solution.py
+++ b/solution.py
@@ -81,7 +81,7 @@
     d = up(y - z, NY, NY)
 
     barrier = pltpu.get_barrier_semaphore()
-    partners = [sib] + zpeer + ypeer + xpeer
+    partners = [sib, zup, zdn, yup, ydn] + xpeer
     for p in partners:
         pl.semaphore_signal(barrier, inc=1, device_id=p, device_id_type=MESH)
 
@@ -197,8 +197,8 @@
         if hop < NZ // 2 - 1:
             put(band.at[:, high], band.at[:, high], zs.at[1, hop], zr.at[high], zdn)
 
-    background = [(3, adjoint_rows), (13, l_rows)]
-    background += [(5 + 3 * h, functools.partial(band_ring, h)) for h in range(NZ // 2 + 1)]
+    background = [(17, adjoint_rows), (13, l_rows)]
+    background += [(at, functools.partial(band_ring, h)) for h, at in enumerate((4, 7, 10, 13, 15))]
 
     def step(n):
         o = pick([st[1] + 4 for st in STEPS], n)
@@ -338,59 +338,56 @@
             lanes = slice(g * W, g * W + W)
             gm[b, :, :, lanes] = (mm_split(a, bb) - fold[b, :, lanes]).reshape(NY, 8, W)
 
-    def plane_reduce_start(b, cond):
-        for s in range(1, NY):
-            to = up(y, s, NY)
-            put(gm.at[b, to], gy.at[b, y], gys.at[b, s], gyr.at[b, y], ypeer[s - 1], cond)
-
     gram(0, xs)
-    plane_reduce_start(0, None)
 
     @pl.when(first)
     def _():
         got(xs2, sib_r.at[NG + 3])
         gram(1, xs2)
 
-    plane_reduce_start(1, first)
-    conds = (None, first)
-
-    def when(cond, fn):
-        if cond is None:
-            fn()
-        else:
-            pl.when(cond)(fn)
-
-    def y_sum(b):
-        gy[b, y] = gm[b, y]
+    sides = ((2, first), (1, k == 1))
+
+    def each(fn):
+        for nb, cond in sides:
+            pl.when(cond)(functools.partial(fn, nb, pl.ds(0, nb)))
+
+    for nb, cond in sides:
+        for s in range(1, NY):
+            to = up(y, s, NY)
+            put(gm.at[pl.ds(0, nb), to], gy.at[pl.ds(0, nb), y], gys.at[s], gyr.at[y], ypeer[s - 1], cond)
+
+    def y_sum(nb, bs):
+        gy[0:nb, y] = gm[0:nb, y]
         for s in range(1, NY):
             frm = up(y, s, NY)
-            got(gy.at[b, frm], gyr.at[b, frm])
-        total = gy[b, 0]
+            got(gy.at[bs, frm], gyr.at[frm])
+        total = gy[0:nb, 0]
         for s in range(1, NY):
-            total = total + gy[b, s]
-        sg[b] = total
-        gx[b, x] = total
-
-    def x_sum(b):
+            total = total + gy[0:nb, s]
+        sg[0:nb] = total
+        gx[0:nb, x] = total
+
+    def x_sum(nb, bs):
         for s in range(1, NX):
             frm = up(x, s, NX)
-            got(gx.at[b, frm], gxr.at[b, frm])
-        total = (gx[b, 0] + gx[b, 1]) + (gx[b, 2] + gx[b, 3])
-        gz[b, 0, z, y] = total[:, 0:W2]
-        gz[b, 1, z, y] = total[:, W2:B]
-
-    def y_wait(b):
+            got(gx.at[bs, frm], gxr.at[frm])
+        total = (gx[0:nb, 0] + gx[0:nb, 1]) + (gx[0:nb, 2] + gx[0:nb, 3])
+        gz[0:nb, 0, z, y] = total[:, :, 0:W2]
+        gz[0:nb, 1, z, y] = total[:, :, W2:B]
+
+    def y_wait(nb, bs):
         for s in range(1, NY):
             frm = up(y, s, NY)
-            got(gz.at[b, 0, z, frm], gar.at[b, frm])
+            got(gz.at[bs, 0, z, frm], gar.at[frm])
         for s in range(1, NZ):
             frm = up(z, s, NZ)
-            got(gz.at[b, 1, frm, y], gbr.at[b, frm])
-
-    for b in range(2):
-        when(conds[b], functools.partial(y_sum, b))
+            got(gz.at[bs, 1, frm, y], gbr.at[frm])
+
+    each(y_sum)
+    for nb, cond in sides:
         for s in range(1, NX):
-            put(sg.at[b], gx.at[b, x], gxs.at[b, s], gxr.at[b, x], xpeer[s - 1], conds[b])
+            put(sg.at[pl.ds(0, nb)], gx.at[pl.ds(0, nb), x], gxs.at[s], gxr.at[x], xpeer[s - 1], cond)
+
     def factor(q):
         return jnp.concatenate([lbuf[p, :, :, 2 * q : 2 * q + 2].reshape(B, 128) for p in range(4)], 1)
 
@@ -418,29 +415,29 @@
 
     between = {0: first_inverse, 2: coupling_factor, 4: tall_rows}
 
-    for b in range(2):
-        when(conds[b], functools.partial(x_sum, b))
+    each(x_sum)
+    for nb, cond in sides:
+        bs = pl.ds(0, nb)
         for s in range(1, NY):
-            put(gz.at[b, 0, z, y], gz.at[b, 0, z, y], gas.at[b, s], gar.at[b, y], ypeer[s - 1], conds[b])
-        for s in range(1, NZ):
-            put(gz.at[b, 1, z, y], gz.at[b, 1, z, y], gbs.at[b, s], gbr.at[b, z], zpeer[s - 1], conds[b])
+            put(gz.at[bs, 0, z, y], gz.at[bs, 0, z, y], gas.at[s], gar.at[y], ypeer[s - 1], cond)
+            put(gz.at[bs, 1, z, y], gz.at[bs, 1, z, y], gbs.at[s], gbr.at[z], zpeer[s - 1], cond)
     second_inverse()
+    each(y_wait)
     for j in range(NZ):
         zz, yy = up(z, ORDER[j], NZ), up(y, ORDER[j], NY)
         hop = abs(ORDER[j])
-        for b in range(2):
-            chunk, other = gz.at[b, 0, zz], gz.at[b, 1, :, yy]
-            if j == 0:
-                when(conds[b], functools.partial(y_wait, b))
-            else:
-                when(conds[b], functools.partial(got, chunk, gzr.at[b, zz]))
-                when(conds[b], functools.partial(got, other, gwr.at[b, yy]))
+        for nb, cond in sides:
+            bs = pl.ds(0, nb)
+            chunk, other = gz.at[bs, 0, zz], gz.at[bs, 1, :, yy]
+            if j > 0:
+                pl.when(cond)(functools.partial(got, chunk, gzr.at[zz]))
+                pl.when(cond)(functools.partial(got, other, gwr.at[yy]))
             if j == 0 or (ORDER[j] < 0 and hop < NZ // 2):
-                put(chunk, chunk, gzs.at[0, b, hop], gzr.at[b, zz], zup, conds[b])
-                put(other, other, gws.at[0, b, hop], gwr.at[b, yy], yup, conds[b])
+                put(chunk, chunk, gzs.at[0, hop], gzr.at[zz], zup, cond)
+                put(other, other, gws.at[0, hop], gwr.at[yy], yup, cond)
             if j == 0 or (ORDER[j] > 0 and hop < NZ // 2 - 1):
-                put(chunk, chunk, gzs.at[1, b, hop], gzr.at[b, zz], zdn, conds[b])
-                put(other, other, gws.at[1, b, hop], gwr.at[b, yy], ydn, conds[b])
+                put(chunk, chunk, gzs.at[1, hop], gzr.at[zz], zdn, cond)
+                put(other, other, gws.at[1, hop], gwr.at[yy], ydn, cond)
         if j in between:
             between[j]()
 
@@ -556,12 +553,12 @@
             dma((2, NG, NZ)), dma((3, NG, NZ)), dma((NG, NX, NZ)),
             dma((NG, NZ)), dma((NG, NZ)),
             dma((NZ,)), dma((NZ,)),
-            dma((2, NY)), dma((2, NY)),
-            dma((2, NX)), dma((2, NX)),
-            dma((2, NY)), dma((2, NY)),
-            dma((2, NZ)), dma((2, NZ)),
-            dma((2, 2, NZ // 2)), dma((2, NZ)),
-            dma((2, 2, NY // 2)), dma((2, NY)),
+            dma((NY,)), dma((NY,)),
+            dma((NX,)), dma((NX,)),
+            dma((NY,)), dma((NY,)),
+            dma((NZ,)), dma((NZ,)),
+            dma((2, NZ // 2)), dma((NZ,)),
+            dma((2, NY // 2)), dma((NY,)),
             dma((NY,)), dma((NY,)),
             dma((2,)), dma((2,)), dma((2,)), dma((2,)),
             dma((NZ,)), dma((NZ,)),
@@ -604,8 +601,21 @@
     out_ref[256:512, 256:512] = wide[1]
 
 
+def store_kernel(*refs):
+    for src, dst in zip(refs[:3], refs[3:]):
+        dst[...] = src[...]
+
+
 def per_device(*args):
-    return panel_call(*args)
+    found = panel_call(*args)
+    vm = pl.BlockSpec(memory_space=pltpu.VMEM)
+    return pl.pallas_call(
+        store_kernel,
+        out_shape=tuple(jax.ShapeDtypeStruct(f.shape, F32) for f in found),
+        in_specs=[vm] * 3,
+        out_specs=(vm,) * 3,
+        name="store",
+    )(*found)
 
 
 def solution(mesh):

time: 148 us -> 147 us (level)
  local copies, waits for them, and re-layouts: 4.19 us -> 0 us
  Pallas kernels: 143 us -> 146 us
    unnamed x3 -> x0, local copies, waits for them, and re-layouts: 4.19 us -> none
    pallas_call x1, Pallas kernels: 143 us -> 144 us  [panel_call(): pl.pallas_call(panel_kernel, out_shape=(jax.ShapeDtypeStruct((ROWS, 2 * B...]
    pallas_call x0 -> x1, Pallas kernels: none -> 1.59 us  [per_device(): pl.pallas_call(store_kernel, out_shape=tuple((jax.ShapeDtypeStruct(f.shap...]
where the time goes in v4:
time: 147 us; the launch traced here: 146 us
  Pallas kernels  146 us (99%)
    pallas_call x1, Pallas kernels, panel_call(): pl.pallas_call(panel_kernel, out_shape=(jax.ShapeDtypeStruct((ROWS, 2 * B...  144 us

profile of v4, /device:TPU:1, one launch (start us, length us, event | category | flops | bytes accessed | tf_op | source)
XLA Modules:
  0.0 146.5 jit_solution(4752204031571427595)
XLA Ops:
  0.6 144.3 %panel_adjoint.1 = (f32[32,1024]{1,0:T(8,128)}, f32[2,16,32]{2,1,0:T(8,128)}, f32[16,32]{1,0:T(8,128)}) custom-call(f32[512,1024]{1,0:T(8,128)} %t_ref.1, f32[32,1024]{1,0:T(8,128)} %r_ref.1, f32[32,1024]{1,0:T(8,128)} %f_ref.1, f32[2,16,512]{2,1,0:T(8,128)} %diag_ref.1, f32[16,512]{1,0:T(8,128)} %cross_ref.1, f32[16,64]{1,0:T(8,128)} %cg_ref.1, f32[16,32]{1,0:T(8,128)} %co_ref.1), custom_call_target="tpu_custom_call" | custom-call | tf_op jit(solution)/shard_map/panel_adjoint/pallas_call | solution.py:512
  144.9 1.6 %store.1 = (f32[32,1024]{1,0:T(8,128)}, f32[2,16,32]{2,1,0:T(8,128)}, f32[16,32]{1,0:T(8,128)}) custom-call(f32[32,1024]{1,0:T(8,128)} %get-tuple-element.6.refs_0_, f32[2,16,32]{2,1,0:T(8,128)} %get-tuple-element.7.refs_1_, f32[16,32]{1,0:T(8,128)} %get-tuple-element.8.refs_2_), custom_call_target="tpu_custom_call" | custom-call | tf_op jit(solution)/shard_map/store/pallas_call | solution.py:612

commit v5 on v4

--- a/solution.py
+++ b/solution.py
@@ -11,9 +11,10 @@
 F32 = jnp.float32
 BF16 = jnp.bfloat16
 NX, NY, NZ = 4, 8, 8
+B = 512
+WIDTHS = (384, 128)
+STARTS = (0, 384)
 NG = 2
-B = 512
-W = B // NG
 W2 = B // 2
 ROWS = 32
 ORDER = (0, -1, 1, -2, 2, -3, 3, -4)
@@ -22,11 +23,6 @@
 LAST0 = NZ - 1
 
 
-def pick(values, n):
-    words = [sum(v << (4 * i) for i, v in enumerate(values[h : h + 8])) for h in (0, 8)]
-    return (jnp.where(n < 8, words[0], words[1]) >> (4 * lax.rem(n, 8))) & 7
-
-
 def split(a):
     hi = a.astype(BF16)
     return hi, (a - hi.astype(F32)).astype(BF16)
@@ -47,8 +43,9 @@
 def panel_kernel(
     t_ref, r_ref, f_ref, diag_ref, cross_ref, cg_ref, co_ref,
     rows_ref, b_ref, c_ref,
-    tbuf, thi, tlo, band, rbuf, psum, sbuf, fbuf, xr, xo, xst, xs, xs2, gm, gy, sg, gx, gz,
-    lloc, cgl, col_, lbuf, cgb, ltr, fold, v1, v2, v1t, v2t, mmat, mt, w1, w2, sbm, cpl, outp,
+    tbuf, thi, tlo, band, rb0, rb1, ps0, ps1, sb0, sb1, fbuf, xr, xo, xst, xs, xs2, gm, gy, sg, gx, gz,
+    lloc, cgl, col_, lbuf, cgb, ltr, fold, v1, v2, v1t, v2t, mmat, mt, w1, w2, sbm, outp,
+    l1t, l2t, l21, v1s, v2s, v2ts, ms,
     sib_s, sib_r, loc, zs, zr, ys, xsm, rr, ss, sr, as_, ar, gys, gyr, gxs, gxr, gas, gar, gbs, gbr, gzs, gzr,
     gws, gwr, lys, lyr, lzs, lzr, lfs, lfr, cs_, cr,
 ):
@@ -60,6 +57,7 @@
     ]
     for c in local:
         c.start()
+    rbuf, psum, sbuf = (rb0, rb1), (ps0, ps1), (sb0, sb1)
     row = lax.axis_index("row")
     col = lax.axis_index("col")
     y, x = row // NX, lax.rem(row, NX)
@@ -95,41 +93,36 @@
     pl.semaphore_wait(barrier, len(partners) + jnp.where(d == 0, 0, 2))
 
     sends = []
-    mode = ["start"]
 
     def put(src, dst, ssem, rsem, target, cond=None):
         c = pltpu.make_async_remote_copy(
             src_ref=src, dst_ref=dst, send_sem=ssem, recv_sem=rsem, device_id=target, device_id_type=MESH
         )
-        act = c.wait_send if mode[0] == "finish" else c.start
         if cond is None:
-            act()
+            c.start()
         else:
-            pl.when(cond)(act)
-        if mode[0] == "start":
-            sends.append((c, cond))
+            pl.when(cond)(c.start)
+        sends.append((c, cond))
 
     def got(ref, sem):
-        if mode[0] != "finish":
-            pltpu.make_async_remote_copy(
-                src_ref=ref, dst_ref=ref, send_sem=sem, recv_sem=sem, device_id=sib, device_id_type=MESH
-            ).wait_recv()
+        pltpu.make_async_remote_copy(
+            src_ref=ref, dst_ref=ref, send_sem=sem, recv_sem=sem, device_id=sib, device_id_type=MESH
+        ).wait_recv()
 
     first = k == 0
-    rcopies = []
+    def rows_of(core, g):
+        return r_ref.at[:, pl.ds(pl.multiple_of(core * B + STARTS[g], 128), WIDTHS[g])]
+
     for g in range(NG):
-        ours = r_ref.at[:, pl.ds(pl.multiple_of(k * B + g * W, 128), W)]
-        theirs = r_ref.at[:, pl.ds(pl.multiple_of((1 - k) * B + g * W, 128), W)]
-        slot, sem = rbuf.at[g, x, z, k], rr.at[g, x, z]
-        put(ours, slot, sib_s.at[NG + 8 + g], sem, swap[0], d != 0)
-        put(theirs, slot, sib_s.at[NG + 10 + g], sem, swap[1])
-        rcopies.append((pltpu.make_async_copy(ours, slot, sem), d == 0))
-        pl.when(d == 0)(rcopies[-1][0].start)
-    for g in range(NG):
-        ours = r_ref.at[:, pl.ds(pl.multiple_of(k * B + g * W, 128), W)]
-        theirs = r_ref.at[:, pl.ds(pl.multiple_of((1 - k) * B + g * W, 128), W)]
-        put(theirs, band.at[g, z, k], sib_s.at[g], sib_r.at[g], sib)
-        pltpu.make_async_copy(ours, band.at[g, z, k], loc.at[5 + g]).start()
+        slot, sem = rbuf[g].at[x, z, k], rr.at[g, x, z]
+        put(rows_of(k, g), slot, sib_s.at[NG + 8 + g], sem, swap[0], d != 0)
+        put(rows_of(1 - k, g), slot, sib_s.at[NG + 10 + g], sem, swap[1])
+        pl.when(d == 0)(pltpu.make_async_copy(rows_of(k, g), slot, sem).start)
+    ours = r_ref.at[:, pl.ds(pl.multiple_of(k * B, 128), B)]
+    theirs = r_ref.at[:, pl.ds(pl.multiple_of((1 - k) * B, 128), B)]
+    put(theirs, band.at[z, k], sib_s.at[0], sib_r.at[0], sib)
+    rcopy = pltpu.make_async_copy(ours, band.at[z, k], loc.at[5])
+    rcopy.start()
     put(t_ref, tbuf.at[k], sib_s.at[NG], sib_r.at[NG], sib)
     tcopy = pltpu.make_async_copy(t_ref, tbuf.at[k], loc.at[0])
     tcopy.start()
@@ -183,103 +176,78 @@
     def band_ring(hop):
         low, high = up(z, -hop, NZ), up(z, hop, NZ)
         if hop == 0:
-            if mode[0] != "finish":
-                for g in range(NG):
-                    ours = band.at[g, z, k]
-                    pltpu.make_async_copy(ours, ours, loc.at[5 + g]).wait()
-                    got(band.at[g, z, 1 - k], sib_r.at[g])
+            rcopy.wait()
+            got(band.at[z, 1 - k], sib_r.at[0])
         else:
-            got(band.at[:, low], zr.at[low])
+            got(band.at[low], zr.at[low])
             if hop < NZ // 2:
-                got(band.at[:, high], zr.at[high])
+                got(band.at[high], zr.at[high])
         if hop < NZ // 2:
-            put(band.at[:, low], band.at[:, low], zs.at[0, hop], zr.at[low], zup)
+            put(band.at[low], band.at[low], zs.at[0, hop], zr.at[low], zup)
         if hop < NZ // 2 - 1:
-            put(band.at[:, high], band.at[:, high], zs.at[1, hop], zr.at[high], zdn)
-
-    background = [(17, adjoint_rows), (13, l_rows)]
-    background += [(at, functools.partial(band_ring, h)) for h, at in enumerate((4, 7, 10, 13, 15))]
-
-    def step(n):
-        o = pick([st[1] + 4 for st in STEPS], n)
-        return pick([st[0] for st in STEPS], n), o, lax.rem(y + o + NZ - 4, NZ)
-
-    def stage_b(n):
-        g, o, zz = step(n)
-        slot, sem = rbuf.at[g, x, zz], rr.at[g, x, zz]
+            put(band.at[high], band.at[high], zs.at[1, hop], zr.at[high], zdn)
+
+    def stage_b(g, o):
+        yy = up(y, o, NY)
+        slot, sem = rbuf[g].at[x, yy], rr.at[g, x, yy]
         got(slot, sem)
-
-        put(slot, slot, ys.at[0, g, o], sem, yup, jnp.logical_and(o >= 1, o <= 4))
-        put(slot, slot, ys.at[1, g, o], sem, ydn, jnp.logical_and(o >= 4, o <= 6))
-        put(slot, slot, xsm.at[0, g, o], sem, xup)
-        put(slot, slot, xsm.at[1, g, o], sem, xdn)
-
-    def stage_d(n):
-        g, o, zz = step(n)
-        left, right = up(x, -1, NX), up(x, 1, NX)
-        got(rbuf.at[g, left, zz], rr.at[g, left, zz])
-        got(rbuf.at[g, right, zz], rr.at[g, right, zz])
-        even = lax.rem(o, 2) == 0
-        chunk = rbuf.at[g, left, zz]
-        put(chunk, chunk, xsm.at[2, g, o], rr.at[g, left, zz], xup, even)
-        chunk = rbuf.at[g, right, zz]
-        put(chunk, chunk, xsm.at[2, g, o], rr.at[g, right, zz], xdn, jnp.logical_not(even))
-
-    def stage_e(n):
-        g, o, zz = step(n)
-        far = up(x, 2, NX)
-        got(rbuf.at[g, far, zz], rr.at[g, far, zz])
-
-    def piece(g, xx):
-        b = split(rbuf[g, xx].reshape(NZ * 2 * ROWS, W))
-        psum[g] += mm_split((thi[xx], tlo[xx]), b).reshape(NZ, 2 * ROWS, W)
+        if -NY // 2 < o <= 0:
+            put(slot, slot, ys.at[0, g, o + 4], sem, yup)
+        if 0 <= o < NY // 2 - 1:
+            put(slot, slot, ys.at[1, g, o + 4], sem, ydn)
+        put(slot, slot, xsm.at[0, g, o + 4], sem, xup)
+        put(slot, slot, xsm.at[1, g, o + 4], sem, xdn)
+
+    left, right, far = up(x, -1, NX), up(x, 1, NX), up(x, 2, NX)
+
+    def stage_d(g, o):
+        yy = up(y, o, NY)
+        got(rbuf[g].at[left, yy], rr.at[g, left, yy])
+        got(rbuf[g].at[right, yy], rr.at[g, right, yy])
+        origin, target = (left, xup) if o % 2 == 0 else (right, xdn)
+        chunk = rbuf[g].at[origin, yy]
+        put(chunk, chunk, xsm.at[2, g, o + 4], rr.at[g, origin, yy], target)
+
+    def stage_e(g, o):
+        yy = up(y, o, NY)
+        got(rbuf[g].at[far, yy], rr.at[g, far, yy])
+
+    def piece(g, xx, fresh):
+        b = split(rbuf[g][xx].reshape(NZ * 2 * ROWS, WIDTHS[g]))
+        part = mm_split((thi[xx], tlo[xx]), b).reshape(NZ, 2 * ROWS, WIDTHS[g])
+        psum[g][...] = part if fresh else psum[g][...] + part
 
     def scatter(g):
         for s in range(1, NZ):
             to = up(z, s, NZ)
-            put(psum.at[g, to], sbuf.at[g, z], ss.at[g, s], sr.at[g, z], zpeer[s - 1])
-        if mode[0] != "finish":
-            sbuf[g, z] = psum[g, z]
-
-    def within(n, fn):
-        @pl.when(jnp.logical_and(n >= 0, n < STEP_COUNT))
-        def _():
-            fn(n)
-
-    def first_group(n):
-        @pl.when(jnp.logical_and(n >= 0, n < NX))
-        def _():
-            piece(0, n)
-
-        @pl.when(n == NX)
-        def _():
-            scatter(0)
-
-    def split_t(h):
-        for i in range(2):
-            thi[2 * h + i], tlo[2 * h + i] = split(tbuf[h, :, 512 * i : 512 * i + 512])
+            put(psum[g].at[to], sbuf[g].at[z], ss.at[g, s], sr.at[g, z], zpeer[s - 1])
+        sbuf[g][z] = psum[g][z]
 
     tcopy.wait()
     got(tbuf.at[1 - k], sib_r.at[NG])
     for h in range(2):
-        split_t(h)
-    psum[...] = jnp.zeros_like(psum)
-    mode[0] = "loop"
-
-    def body(i, carry):
-        within(i, stage_b)
-        within(i - lag_d, stage_d)
-        within(i - lag_e, stage_e)
-        for at, task in background:
-            pl.when(i == at)(task)
-        first_group(i - lag_e - LAST0 - 1)
-        return carry
-
-    lax.fori_loop(0, STEP_COUNT + 4, body, 0)
-    mode[0] = "start"
+        for i in range(2):
+            thi[2 * h + i], tlo[2 * h + i] = split(tbuf[h, :, 512 * i : 512 * i + 512])
+
+    after = {i: [] for i in range(STEP_COUNT + lag_e)}
+    for h, at in enumerate((4, 7, 10, 13, 15)):
+        after[at].append(functools.partial(band_ring, h))
+    after[13].append(l_rows)
+    after[17].append(adjoint_rows)
+    for xx in range(NX):
+        after[LAST0 + lag_e + 1 + xx].append(functools.partial(piece, 0, xx, xx == 0))
+    after[LAST0 + lag_e + 5].append(functools.partial(scatter, 0))
+    after[STEP_COUNT].append(functools.partial(piece, 1, x, True))
+    after[STEP_COUNT + lag_d].append(functools.partial(piece, 1, left, False))
+    after[STEP_COUNT + lag_d].append(functools.partial(piece, 1, right, False))
+    for i in range(STEP_COUNT + lag_e):
+        for lag, stage in ((0, stage_b), (lag_d, stage_d), (lag_e, stage_e)):
+            if 0 <= i - lag < STEP_COUNT:
+                stage(*STEPS[i - lag])
+        for task in after[i]:
+            task()
     l_planes()
-    for xx in range(NX):
-        piece(1, xx)
+    piece(1, far, False)
     scatter(1)
     l_far()
 
@@ -309,12 +277,12 @@
     for g in range(NG):
         for s in range(1, NZ):
             frm = up(z, s, NZ)
-            got(sbuf.at[g, frm], sr.at[g, frm])
-        total = sbuf[g, 0]
+            got(sbuf[g].at[frm], sr.at[g, frm])
+        total = sbuf[g][0]
         for s in range(1, NZ):
-            total = total + sbuf[g, s]
-        lanes = slice(g * W, g * W + W)
-        xr[:, :, lanes] = fbuf[:, :, lanes] - 2.0 * total.reshape(2, ROWS, W)
+            total = total + sbuf[g][s]
+        lanes = slice(STARTS[g], STARTS[g] + WIDTHS[g])
+        xr[:, :, lanes] = fbuf[:, :, lanes] - 2.0 * total.reshape(2, ROWS, WIDTHS[g])
 
     xall = xr[...].reshape(2 * ROWS, B)
     for s in range(NZ):
@@ -333,10 +301,7 @@
 
     def gram(b, src):
         a = split(src[...].reshape(NZ * 64, 64).T)
-        for g in range(NG):
-            bb = split(band[g].reshape(NZ * 64, W))
-            lanes = slice(g * W, g * W + W)
-            gm[b, :, :, lanes] = (mm_split(a, bb) - fold[b, :, lanes]).reshape(NY, 8, W)
+        gm[b] = (mm_split(a, split(band[...].reshape(B, B))) - fold[b]).reshape(NY, 8, B)
 
     gram(0, xs)
 
@@ -403,11 +368,18 @@
         invert(tile(0), v1)
 
     def coupling_factor():
+        l2t[0], l2t[1] = split(factor(1).T)
+        l1t[0], l1t[1] = split(factor(0).T)
+        l21[0], l21[1] = split(factor(2))
+        v1s[0], v1s[1] = split(v1[...])
+        v2s[0], v2s[1] = split(v2[...])
+        v2ts[0], v2ts[1] = split(v2t[...])
         v1t[...] = v1[...].T
         mmat[...] = mm(factor(2), v1[...])
 
     def tall_rows():
         mt[...] = mmat[...].T
+        ms[0], ms[1] = split(mmat[...])
         got(xo.at[1 - k], sib_r.at[NG + 2])
         h2 = mm(xo[1], v2[...])
         rows_ref[:, B : 2 * B] = h2
@@ -453,27 +425,26 @@
 
     @pl.when(k == 1)
     def _():
-        left = split(v2t[...])
-        p2 = mm_split(left, split(gram_total(0)))
-        q2 = lowered(mm(factor(1).T, jnp.where(r >= c, -p2, 0.0)))
-        w1[...] = mm(q2 + q2.T, v2[...])
-        sbm[...] = 0.5 * mm_split(left, split(w1[...]))
+        p2 = mm_split(v2ts, split(gram_total(0)))
+        q2 = lowered(mm_split(l2t, split(jnp.where(r >= c, -p2, 0.0))))
+        w1[...] = mm_split(split(q2 + q2.T), v2s)
+        sbm[...] = 0.5 * mm_split(v2ts, split(w1[...]))
 
     put(sbm, sbm, sib_s.at[NG + 6], sib_r.at[NG + 6], sib, k == 1)
 
     @pl.when(first)
     def _():
-        p1 = split(-mm(v2t[...], gram_total(1)))
-        w1[...] = mm_split(p1, split(v1[...]))
+        p1 = split(-mm_split(v2ts, split(gram_total(1))))
+        w1[...] = mm_split(p1, v1s)
         w2[...] = mm(v1t[...], gram_total(0)) + mm_split(split(mt[...]), p1)
         got(sbm, sib_r.at[NG + 6])
-        coupling = w1[...] - 2.0 * mm(sbm[...], mmat[...])
-        cpl[...] = coupling
-        outp[0] = cpl[own, :]
-        grad = jnp.where(r >= c, -w2[...] - mm(coupling.T, factor(2)), 0.0)
-        q1 = lowered(mm(factor(0).T, grad))
+        coupling = w1[...] - 2.0 * mm_split(split(sbm[...]), ms)
+        w1[...] = coupling
+        outp[0] = w1[own, :]
+        grad = jnp.where(r >= c, -w2[...] - mm_split(split(coupling.T), l21), 0.0)
+        q1 = lowered(mm_split(l1t, split(grad)))
         w1[...] = q1 + q1.T
-        outp[1] = 0.5 * mm(mm(v1t[own, :], w1[...]), v1[...])
+        outp[1] = 0.5 * mm_split(split(mm(v1t[own, :], w1[...])), v1s)
 
     put(outp, outp, sib_s.at[NG + 7], sib_r.at[NG + 7], sib, first)
 
@@ -491,17 +462,6 @@
             c.wait_send()
         else:
             pl.when(cond)(c.wait_send)
-    mode[0] = "finish"
-    for _, task in background:
-        task()
-    scatter(0)
-
-    def sent(n, carry):
-        stage_b(n)
-        stage_d(n)
-        return carry
-
-    lax.fori_loop(0, STEP_COUNT, sent, 0)
 
 
 def panel_call(*args):
@@ -522,10 +482,12 @@
             pltpu.VMEM((2, 512, 1024), F32),
             pltpu.VMEM((NX, 512, 512), BF16),
             pltpu.VMEM((NX, 512, 512), BF16),
-            pltpu.VMEM((NG, NZ, 2, ROWS, W), F32),
-            pltpu.VMEM((NG, NX, NZ, 2, ROWS, W), F32),
-            pltpu.VMEM((NG, NZ, 2 * ROWS, W), F32),
-            pltpu.VMEM((NG, NZ, 2 * ROWS, W), F32),
+            pltpu.VMEM((NZ, 2, ROWS, B), F32),
+        ]
+        + [pltpu.VMEM((NX, NZ, 2, ROWS, w), F32) for w in WIDTHS]
+        + [pltpu.VMEM((NZ, 2 * ROWS, w), F32) for w in WIDTHS]
+        + [pltpu.VMEM((NZ, 2 * ROWS, w), F32) for w in WIDTHS]
+        + [
             pltpu.VMEM((2, ROWS, B), F32),
             pltpu.VMEM((2, ROWS, B), F32),
             pltpu.VMEM((2, ROWS, B), F32),
@@ -545,9 +507,10 @@
             pltpu.VMEM((3, B, 16), F32),
             pltpu.VMEM((2, 64, B), F32),
         ]
-        + [square] * 10
+        + [square] * 9
+        + [pltpu.VMEM((2, 16, B), F32)]
+        + [pltpu.VMEM((2, B, B), BF16)] * 7
         + [
-            pltpu.VMEM((2, 16, B), F32),
             dma((NG + 12,)), dma((NG + 8,)), dma((NG + 6,)),
             dma((2, NZ)), dma((NZ,)),
             dma((2, NG, NZ)), dma((3, NG, NZ)), dma((NG, NX, NZ)),

time: 147 us -> 155 us (1.054)
  Pallas kernels: 146 us -> 154 us
    pallas_call x1, Pallas kernels: 144 us -> 152 us  [panel_call(): pl.pallas_call(panel_kernel, out_shape=(jax.ShapeDtypeStruct((ROWS, 2 * B...]
where the time goes in v5:
time: 155 us
  Pallas kernels  154 us (99%)
    pallas_call x1, Pallas kernels, panel_call(): pl.pallas_call(panel_kernel, out_shape=(jax.ShapeDtypeStruct((ROWS, 2 * B...  152 us

profile of v5, /device:TPU:1, one launch (start us, length us, event | category | flops | bytes accessed | tf_op | source)
XLA Modules:
  0.0 154.6 jit_solution(6003427562187396313)
XLA Ops:
  0.6 152.4 %panel_adjoint.1 = (f32[32,1024]{1,0:T(8,128)}, f32[2,16,32]{2,1,0:T(8,128)}, f32[16,32]{1,0:T(8,128)}) custom-call(f32[512,1024]{1,0:T(8,128)} %t_ref.1, f32[32,1024]{1,0:T(8,128)} %r_ref.1, f32[32,1024]{1,0:T(8,128)} %f_ref.1, f32[2,16,512]{2,1,0:T(8,128)} %diag_ref.1, f32[16,512]{1,0:T(8,128)} %cross_ref.1, f32[16,64]{1,0:T(8,128)} %cg_ref.1, f32[16,32]{1,0:T(8,128)} %co_ref.1), custom_call_target="tpu_custom_call" | custom-call | tf_op jit(solution)/shard_map/panel_adjoint/pallas_call | solution.py:472
  153.0 1.6 %store.1 = (f32[32,1024]{1,0:T(8,128)}, f32[2,16,32]{2,1,0:T(8,128)}, f32[16,32]{1,0:T(8,128)}) custom-call(f32[32,1024]{1,0:T(8,128)} %get-tuple-element.6.refs_0_, f32[2,16,32]{2,1,0:T(8,128)} %get-tuple-element.7.refs_1_, f32[16,32]{1,0:T(8,128)} %get-tuple-element.8.refs_2_), custom_call_target="tpu_custom_call" | custom-call | tf_op jit(solution)/shard_map/store/pallas_call | solution.py:575

commit v6 on v5

--- a/solution.py
+++ b/solution.py
@@ -12,8 +12,8 @@
 BF16 = jnp.bfloat16
 NX, NY, NZ = 4, 8, 8
 B = 512
-WIDTHS = (384, 128)
-STARTS = (0, 384)
+WIDTHS = (256, 256)
+STARTS = (0, 256)
 NG = 2
 W2 = B // 2
 ROWS = 32
@@ -170,8 +170,8 @@
         for s in range(1, NZ):
             put(cgb.at[z], cgb.at[z], cs_.at[s], cr.at[z], zpeer[s - 1])
 
-    lag_d = 2
-    lag_e = 4
+    lag_d = 4
+    lag_e = 8
 
     def band_ring(hop):
         low, high = up(z, -hop, NZ), up(z, hop, NZ)

time: 155 us -> 147 us (0.948)
  Pallas kernels: 154 us -> 146 us
    pallas_call x1, Pallas kernels: 152 us -> 144 us  [panel_call(): pl.pallas_call(panel_kernel, out_shape=(jax.ShapeDtypeStruct((ROWS, 2 * B...]
where the time goes in v6:
time: 147 us
  Pallas kernels  146 us (99%)
    pallas_call x1, Pallas kernels, panel_call(): pl.pallas_call(panel_kernel, out_shape=(jax.ShapeDtypeStruct((ROWS, 2 * B...  144 us

profile of v6, /device:TPU:1, one launch (start us, length us, event | category | flops | bytes accessed | tf_op | source)
XLA Modules:
  0.0 146.7 jit_solution(3728292888831487213)
XLA Ops:
  0.6 144.5 %panel_adjoint.1 = (f32[32,1024]{1,0:T(8,128)}, f32[2,16,32]{2,1,0:T(8,128)}, f32[16,32]{1,0:T(8,128)}) custom-call(f32[512,1024]{1,0:T(8,128)} %t_ref.1, f32[32,1024]{1,0:T(8,128)} %r_ref.1, f32[32,1024]{1,0:T(8,128)} %f_ref.1, f32[2,16,512]{2,1,0:T(8,128)} %diag_ref.1, f32[16,512]{1,0:T(8,128)} %cross_ref.1, f32[16,64]{1,0:T(8,128)} %cg_ref.1, f32[16,32]{1,0:T(8,128)} %co_ref.1), custom_call_target="tpu_custom_call" | custom-call | tf_op jit(solution)/shard_map/panel_adjoint/pallas_call | solution.py:472
  145.1 1.6 %store.1 = (f32[32,1024]{1,0:T(8,128)}, f32[2,16,32]{2,1,0:T(8,128)}, f32[16,32]{1,0:T(8,128)}) custom-call(f32[32,1024]{1,0:T(8,128)} %get-tuple-element.6.refs_0_, f32[2,16,32]{2,1,0:T(8,128)} %get-tuple-element.7.refs_1_, f32[16,32]{1,0:T(8,128)} %get-tuple-element.8.refs_2_), custom_call_target="tpu_custom_call" | custom-call | tf_op jit(solution)/shard_map/store/pallas_call | solution.py:575

commit v7 on v6

--- a/solution.py
+++ b/solution.py
@@ -45,7 +45,7 @@
     rows_ref, b_ref, c_ref,
     tbuf, thi, tlo, band, rb0, rb1, ps0, ps1, sb0, sb1, fbuf, xr, xo, xst, xs, xs2, gm, gy, sg, gx, gz,
     lloc, cgl, col_, lbuf, cgb, ltr, fold, v1, v2, v1t, v2t, mmat, mt, w1, w2, sbm, outp,
-    l1t, l2t, l21, v1s, v2s, v2ts, ms,
+    l1t, l2t, l21, v1s, v2s, v2ts, ms, bsp,
     sib_s, sib_r, loc, zs, zr, ys, xsm, rr, ss, sr, as_, ar, gys, gyr, gxs, gxr, gas, gar, gbs, gbr, gzs, gzr,
     gws, gwr, lys, lyr, lzs, lzr, lfs, lfr, cs_, cr,
 ):
@@ -272,6 +272,7 @@
     def _():
         fold[0] = mm(ltr[1, mine, :], cross_half(NZ))
 
+    bsp[0], bsp[1] = split(band[...].reshape(B, B))
     fcopy.wait()
     got(fbuf.at[1 - k], sib_r.at[NG + 1])
     for g in range(NG):
@@ -290,7 +291,6 @@
     for s in range(1, NZ):
         to = up(z, s, NZ)
         put(xst.at[to], xs.at[z], as_.at[s], ar.at[z], zpeer[s - 1])
-    l_cores()
     put(xr.at[1 - k], xo.at[k], sib_s.at[NG + 2], sib_r.at[NG + 2], sib)
     xo[k] = xr[k]
     xs[z] = xst[z]
@@ -301,7 +301,7 @@
 
     def gram(b, src):
         a = split(src[...].reshape(NZ * 64, 64).T)
-        gm[b] = (mm_split(a, split(band[...].reshape(B, B))) - fold[b]).reshape(NY, 8, B)
+        gm[b] = (mm_split(a, bsp) - fold[b]).reshape(NY, 8, B)
 
     gram(0, xs)
 
@@ -320,6 +320,8 @@
         for s in range(1, NY):
             to = up(y, s, NY)
             put(gm.at[pl.ds(0, nb), to], gy.at[pl.ds(0, nb), y], gys.at[s], gyr.at[y], ypeer[s - 1], cond)
+
+    l_cores()
 
     def y_sum(nb, bs):
         gy[0:nb, y] = gm[0:nb, y]
@@ -509,7 +511,7 @@
         ]
         + [square] * 9
         + [pltpu.VMEM((2, 16, B), F32)]
-        + [pltpu.VMEM((2, B, B), BF16)] * 7
+        + [pltpu.VMEM((2, B, B), BF16)] * 8
         + [
             dma((NG + 12,)), dma((NG + 8,)), dma((NG + 6,)),
             dma((2, NZ)), dma((NZ,)),

time: 147 us -> 147 us (level)
  no operation moved by 1% of the time
where the time goes in v7:
time: 147 us
  Pallas kernels  146 us (99%)
    pallas_call x1, Pallas kernels, panel_call(): pl.pallas_call(panel_kernel, out_shape=(jax.ShapeDtypeStruct((ROWS, 2 * B...  144 us

profile of v7, /device:TPU:1, one launch (start us, length us, event | category | flops | bytes accessed | tf_op | source)
XLA Modules:
  0.0 146.7 jit_solution(13028309739884502839)
XLA Ops:
  0.6 144.4 %panel_adjoint.1 = (f32[32,1024]{1,0:T(8,128)}, f32[2,16,32]{2,1,0:T(8,128)}, f32[16,32]{1,0:T(8,128)}) custom-call(f32[512,1024]{1,0:T(8,128)} %t_ref.1, f32[32,1024]{1,0:T(8,128)} %r_ref.1, f32[32,1024]{1,0:T(8,128)} %f_ref.1, f32[2,16,512]{2,1,0:T(8,128)} %diag_ref.1, f32[16,512]{1,0:T(8,128)} %cross_ref.1, f32[16,64]{1,0:T(8,128)} %cg_ref.1, f32[16,32]{1,0:T(8,128)} %co_ref.1), custom_call_target="tpu_custom_call" | custom-call | tf_op jit(solution)/shard_map/panel_adjoint/pallas_call | solution.py:474
  145.1 1.6 %store.1 = (f32[32,1024]{1,0:T(8,128)}, f32[2,16,32]{2,1,0:T(8,128)}, f32[16,32]{1,0:T(8,128)}) custom-call(f32[32,1024]{1,0:T(8,128)} %get-tuple-element.6.refs_0_, f32[2,16,32]{2,1,0:T(8,128)} %get-tuple-element.7.refs_1_, f32[16,32]{1,0:T(8,128)} %get-tuple-element.8.refs_2_), custom_call_target="tpu_custom_call" | custom-call | tf_op jit(solution)/shard_map/store/pallas_call | solution.py:577

commit v8 on v4

--- a/solution.py
+++ b/solution.py
@@ -413,7 +413,7 @@
         rows_ref[:, B : 2 * B] = h2
         rows_ref[:, 0:B] = mm(xo[0], v1[...]) - mm(h2, mmat[...])
 
-    between = {0: first_inverse, 2: coupling_factor, 4: tall_rows}
+    between = {0: second_inverse, 2: first_inverse, 4: coupling_factor, 6: tall_rows}
 
     each(x_sum)
     for nb, cond in sides:
@@ -421,7 +421,6 @@
         for s in range(1, NY):
             put(gz.at[bs, 0, z, y], gz.at[bs, 0, z, y], gas.at[s], gar.at[y], ypeer[s - 1], cond)
             put(gz.at[bs, 1, z, y], gz.at[bs, 1, z, y], gbs.at[s], gbr.at[z], zpeer[s - 1], cond)
-    second_inverse()
     each(y_wait)
     for j in range(NZ):
         zz, yy = up(z, ORDER[j], NZ), up(y, ORDER[j], NY)

time: 147 us -> 147 us (level)
  no operation moved by 1% of the time
where the time goes in v8:
time: 147 us
  Pallas kernels  146 us (99%)
    pallas_call x1, Pallas kernels, panel_call(): pl.pallas_call(panel_kernel, out_shape=(jax.ShapeDtypeStruct((ROWS, 2 * B...  145 us

profile of v8, /device:TPU:1, one launch (start us, length us, event | category | flops | bytes accessed | tf_op | source)
XLA Modules:
  0.0 146.8 jit_solution(14987690786316444917)
XLA Ops:
  0.6 144.5 %panel_adjoint.1 = (f32[32,1024]{1,0:T(8,128)}, f32[2,16,32]{2,1,0:T(8,128)}, f32[16,32]{1,0:T(8,128)}) custom-call(f32[512,1024]{1,0:T(8,128)} %t_ref.1, f32[32,1024]{1,0:T(8,128)} %r_ref.1, f32[32,1024]{1,0:T(8,128)} %f_ref.1, f32[2,16,512]{2,1,0:T(8,128)} %diag_ref.1, f32[16,512]{1,0:T(8,128)} %cross_ref.1, f32[16,64]{1,0:T(8,128)} %cg_ref.1, f32[16,32]{1,0:T(8,128)} %co_ref.1), custom_call_target="tpu_custom_call" | custom-call | tf_op jit(solution)/shard_map/panel_adjoint/pallas_call | solution.py:511
  145.2 1.6 %store.1 = (f32[32,1024]{1,0:T(8,128)}, f32[2,16,32]{2,1,0:T(8,128)}, f32[16,32]{1,0:T(8,128)}) custom-call(f32[32,1024]{1,0:T(8,128)} %get-tuple-element.6.refs_0_, f32[2,16,32]{2,1,0:T(8,128)} %get-tuple-element.7.refs_1_, f32[16,32]{1,0:T(8,128)} %get-tuple-element.8.refs_2_), custom_call_target="tpu_custom_call" | custom-call | tf_op jit(solution)/shard_map/store/pallas_call | solution.py:611
